TPU v7x, 512 devices: a whole 4x8x8 slice. The times are simulated.
512 devices in a mesh: wide: 64 (over y, x, z_lo), narrow: 8 (over z_hi, core).
Axes of the slice: x: 4, y: 8, z: 8 (z_hi: 4, z_lo: 2; z = z_hi * 2 + z_lo), core: 2. Of those that a mesh axis runs over, the one named last changes fastest.
Arguments:
- tval: bfloat16 [4096, 12, 128, 128], P(('wide', 'narrow')), may hold values from -0.16992188 to 0.16992188
- tcol: int32 [4096, 12], replicated, may hold values from 0 to 4095, as said below
- ocol: int32 [4096, 12], P(('wide', 'narrow')), may hold values from 0 to 4095, as said below
- basis: bfloat16 [524288, 128], P(('wide', 'narrow')), may hold values from -6 to 6
Outputs:
- projected: bfloat16 [524288, 128], P(('wide', 'narrow'))
- level: float32 [128, 128], replicated
Inputs may be any that keep to these rules, and one draw needn't show every extreme that they name: `tcol`: the 12 block columns of row i are distinct, include i, and each lies within cyclic distance 8 of i modulo 4096. `ocol`: the 12 block columns of row i are distinct, include i, and each lies within cyclic distance 8 of i modulo 4096.
All inputs are finite; a program needn't handle non-finite values.
Results may differ from a plain program's by a relative error of at most 0.0049.
Values may be sent and summed in bfloat16 or wider, within the bound.
No kernel may reach another device: no remote copies, remote signals or barrier semaphores. Data moves between devices by JAX's collectives and lax.ppermute only.
A program may use at most 64 MiB of HBM per device.

v0:
```python
import jax
import jax.numpy as jnp
from jax import lax
from jax.sharding import PartitionSpec as P


def with_halo(cells, sides, width):
    for axis, dim in sides:
        count = lax.axis_size(axis)
        head = lax.slice_in_dim(cells, 0, width, axis=dim)
        tail = lax.slice_in_dim(cells, cells.shape[dim] - width, cells.shape[dim], axis=dim)
        cells = jnp.concatenate(
            [
                lax.ppermute(tail, axis, [(i, (i + 1) % count) for i in range(count)]),
                cells,
                lax.ppermute(head, axis, [((i + 1) % count, i) for i in range(count)]),
            ],
            axis=dim,
        )
    return cells


def per_device(tval, tcol, ocol, basis):
    local = tval.shape[0]
    size = tval.shape[2]
    width = basis.shape[1]
    slots = tval.shape[1]
    devices = lax.axis_size(("wide", "narrow"))
    count = local * devices
    first = lax.axis_index(("wide", "narrow")) * local
    extended = with_halo(tval, ((("wide", "narrow"), 0),), local)
    basis_ext = with_halo(basis, ((("wide", "narrow"), 0),), local * size)
    basis_blocks = basis_ext.reshape(3 * local, size, width)
    slot_ids = jnp.arange(slots, dtype=jnp.int32)

    def one_row(index):
        glob = first + index
        cols = tcol[glob]
        places = (cols - first + local) % count
        pattern = tcol[cols]
        outcols = ocol[index]
        match = (pattern[None, :, :] == outcols[:, None, None]).astype(jnp.int32)
        which = jnp.sum(match * slot_ids[None, None, :], axis=2)
        valid = jnp.sum(match, axis=2).astype(jnp.bfloat16)
        chosen = extended[places[None, :], which]
        selected = chosen * valid[:, :, None, None]
        square = jnp.einsum(
            "sab,osbc->oac", tval[index], selected, preferred_element_type=jnp.float32
        ).astype(jnp.bfloat16)
        picked = basis_blocks[(outcols - first + local) % count]
        result = jnp.einsum("oac,ock->ak", square, picked, preferred_element_type=jnp.float32)
        return result.astype(jnp.bfloat16)

    projected = lax.map(one_row, jnp.arange(local, dtype=jnp.int32)).reshape(local * size, width)
    partial_level = jnp.dot(basis.T, projected, preferred_element_type=jnp.float32)
    level = lax.psum(partial_level, ("wide", "narrow"))
    level = level / jnp.sqrt(jnp.float32(count * size))
    return (projected, level)


def solution(mesh):
    return jax.shard_map(
        per_device,
        mesh=mesh,
        in_specs=(
            P(("wide", "narrow"), None, None, None),
            P(),
            P(("wide", "narrow"), None),
            P(("wide", "narrow"), None),
        ),
        out_specs=(P(("wide", "narrow"), None), P()),
        check_vma=False,
    )
```

profile of v0, /device:TPU:1, one launch (start us, length us, event | category | flops | bytes accessed | tf_op | source)
XLA Modules:
  0.0 651.2 jit_solution(2711179265260050932)
XLA Ops:
  7.2 7.2 %collective-permute-start = (bf16[8,12,128,128]{3,2,1,0:T(8,128)(2,1)}, bf16[8,12,128,128]{3,2,1,0:T(8,128)(2,1)}, u32[]{:S(2)}, u32[]{:S(2)}) collective-permute-start(bf16[8,12,128,128]{3,2,1,0:T(8,128)(2,1)} %param.6), channel_id=1, source_target_pairs={{0,1},{1,2},{2,3},{3,4},{4,5},{5,6},{6,7},{7,8},{8,9},{9,10},{10,1... | collective-permute-start | bytes 9437192 | tf_op jit(solution)/shard_map/ppermute | solution.py:14
  14.4 3.5 collective-permute-start.1
  17.9 3.0 collective-permute-start.2
  20.9 9.1 %collective-permute-start.3 = (bf16[1024,128]{1,0:T(8,128)(2,1)}, bf16[1024,128]{1,0:T(8,128)(2,1)S(1)}, u32[]{:S(2)}, u32[]{:S(2)}) collective-permute-start(bf16[1024,128]{1,0:T(8,128)(2,1)} %param.9), channel_id=1, source_target_pairs={{1,0},{2,1},{3,2},{4,3},{5,4},{6,5},{7,6},{8,7},{9,8},{10,9},{11,1... | collective-permute-start | bytes 786440 | tf_op jit(solution)/shard_map/ppermute | solution.py:16
  30.0 1.6 copy.12
  31.6 55.9 %collective-permute-done.2 = bf16[1024,128]{1,0:T(8,128)(2,1)S(1)} collective-permute-done((bf16[1024,128]{1,0:T(8,128)(2,1)}, bf16[1024,128]{1,0:T(8,128)(2,1)S(1)}, u32[]{:S(2)}, u32[]{:S(2)}) %collective-permute-start.2) | collective-permute-done | bytes 262176 | tf_op jit(solution)/shard_map/ppermute | solution.py:14
  87.5 6.0 collective-permute-done.3
  93.5 1.0 pad_maximum_fusion.1
  94.5 7.7 %pad_maximum_fusion = bf16[24,12,128,128]{3,2,1,0:T(8,128)(2,1)} fusion(bf16[8,12,128,128]{3,2,1,0:T(8,128)(2,1)} %collective-permute-done.1, bf16[8,12,128,128]{3,2,1,0:T(8,128)(2,1)} %param.6, bf16[8,12,128,128]{3,2,1,0:T(8,128)(2,1)} %collective-permute-done), kind=kLoop, calls=%fused_computation.47 | loop fusion | flops 9437184 | bytes 18874368 | tf_op jit(solution)/shard_map/concatenate | solution.py:12
  102.2 269.7 %while.13 = (s32[]{:T(128)}, bf16[8,128,128]{2,1,0:T(8,128)(2,1)}, s32[8]{0:T(128)S(1)}, s32[]{:T(128)}, s32[4096,12]{1,0:T(8,128)S(1)}, /*index=5*/s32[8,12]{1,...) while((s32[]{:T(128)}, bf16[8,128,128]{2,1,0:T(8,128)(2,1)}, ...), condition=%wide.region_3.4_spmd.clone, body=%wide.region_0.3_spmd.clone.sunk | while | flops 656895552 | bytes 25215700 | solution.py:54
  102.2 0.6 dynamic_slice.51
  105.4 0.7 fusion.62
  106.6 0.7 fusion.63
  108.0 15.8 %gather_fusion.2 = bf16[144,128,128]{2,1,0:T(8,128)(2,1)} fusion(bf16[24,12,128,128]{3,2,1,0:T(8,128)(2,1)} %get-tuple-element.305, s32[144]{0:T(256)S(1)} %reshape.191), kind=kCustom, calls=%fused_computation.1.clone.clone.1 | custom fusion | bytes 9438336 | tf_op jit(solution)/shard_map/while/body/eval_jaxpr/gather | solution.py:45
  123.8 6.7 %copy.17 = bf16[12,12,128,128]{2,3,1,0:T(8,128)(2,1)} copy(bf16[12,12,128,128]{3,2,1,0:T(8,128)(2,1)} %bitcast.95) | data formatting | bytes 9437184 | tf_op jit(solution)/shard_map/while/body/eval_jaxpr/gather | solution.py:45
  130.5 0.6 gather_fusion
  131.2 4.8 fusion.66
  135.9 0.6 dynamic_slice.51
  139.1 0.7 fusion.62
  140.3 0.7 fusion.63
  141.7 15.8 %gather_fusion.2 = bf16[144,128,128]{2,1,0:T(8,128)(2,1)} fusion(bf16[24,12,128,128]{3,2,1,0:T(8,128)(2,1)} %get-tuple-element.305, s32[144]{0:T(256)S(1)} %reshape.191), kind=kCustom, calls=%fused_computation.1.clone.clone.1 | custom fusion | bytes 9438336 | tf_op jit(solution)/shard_map/while/body/eval_jaxpr/gather | solution.py:45
  157.6 6.7 %copy.17 = bf16[12,12,128,128]{2,3,1,0:T(8,128)(2,1)} copy(bf16[12,12,128,128]{3,2,1,0:T(8,128)(2,1)} %bitcast.95) | data formatting | bytes 9437184 | tf_op jit(solution)/shard_map/while/body/eval_jaxpr/gather | solution.py:45
  164.2 0.6 gather_fusion
  164.9 4.8 fusion.66
  169.6 0.6 dynamic_slice.51
  172.8 0.7 fusion.62
  174.1 0.7 fusion.63
  175.4 15.8 %gather_fusion.2 = bf16[144,128,128]{2,1,0:T(8,128)(2,1)} fusion(bf16[24,12,128,128]{3,2,1,0:T(8,128)(2,1)} %get-tuple-element.305, s32[144]{0:T(256)S(1)} %reshape.191), kind=kCustom, calls=%fused_computation.1.clone.clone.1 | custom fusion | bytes 9438336 | tf_op jit(solution)/shard_map/while/body/eval_jaxpr/gather | solution.py:45
  191.3 6.7 %copy.17 = bf16[12,12,128,128]{2,3,1,0:T(8,128)(2,1)} copy(bf16[12,12,128,128]{3,2,1,0:T(8,128)(2,1)} %bitcast.95) | data formatting | bytes 9437184 | tf_op jit(solution)/shard_map/while/body/eval_jaxpr/gather | solution.py:45
  198.6 4.8 fusion.66
  203.4 0.6 dynamic_slice.51
  206.5 0.7 fusion.62
  207.8 0.7 fusion.63
  209.1 15.8 %gather_fusion.2 = bf16[144,128,128]{2,1,0:T(8,128)(2,1)} fusion(bf16[24,12,128,128]{3,2,1,0:T(8,128)(2,1)} %get-tuple-element.305, s32[144]{0:T(256)S(1)} %reshape.191), kind=kCustom, calls=%fused_computation.1.clone.clone.1 | custom fusion | bytes 9438336 | tf_op jit(solution)/shard_map/while/body/eval_jaxpr/gather | solution.py:45
  225.0 6.7 %copy.17 = bf16[12,12,128,128]{2,3,1,0:T(8,128)(2,1)} copy(bf16[12,12,128,128]{3,2,1,0:T(8,128)(2,1)} %bitcast.95) | data formatting | bytes 9437184 | tf_op jit(solution)/shard_map/while/body/eval_jaxpr/gather | solution.py:45
  232.3 4.8 fusion.66
  237.1 0.6 dynamic_slice.51
  240.2 0.7 fusion.62
  241.5 0.7 fusion.63
  242.8 15.8 %gather_fusion.2 = bf16[144,128,128]{2,1,0:T(8,128)(2,1)} fusion(bf16[24,12,128,128]{3,2,1,0:T(8,128)(2,1)} %get-tuple-element.305, s32[144]{0:T(256)S(1)} %reshape.191), kind=kCustom, calls=%fused_computation.1.clone.clone.1 | custom fusion | bytes 9438336 | tf_op jit(solution)/shard_map/while/body/eval_jaxpr/gather | solution.py:45
  258.7 6.7 %copy.17 = bf16[12,12,128,128]{2,3,1,0:T(8,128)(2,1)} copy(bf16[12,12,128,128]{3,2,1,0:T(8,128)(2,1)} %bitcast.95) | data formatting | bytes 9437184 | tf_op jit(solution)/shard_map/while/body/eval_jaxpr/gather | solution.py:45
  266.0 4.8 fusion.66
  270.8 0.6 dynamic_slice.51
  273.9 0.7 fusion.62
  275.2 0.7 fusion.63
  276.5 15.8 %gather_fusion.2 = bf16[144,128,128]{2,1,0:T(8,128)(2,1)} fusion(bf16[24,12,128,128]{3,2,1,0:T(8,128)(2,1)} %get-tuple-element.305, s32[144]{0:T(256)S(1)} %reshape.191), kind=kCustom, calls=%fused_computation.1.clone.clone.1 | custom fusion | bytes 9438336 | tf_op jit(solution)/shard_map/while/body/eval_jaxpr/gather | solution.py:45
  292.4 6.7 %copy.17 = bf16[12,12,128,128]{2,3,1,0:T(8,128)(2,1)} copy(bf16[12,12,128,128]{3,2,1,0:T(8,128)(2,1)} %bitcast.95) | data formatting | bytes 9437184 | tf_op jit(solution)/shard_map/while/body/eval_jaxpr/gather | solution.py:45
  299.7 4.8 fusion.66
  304.5 0.6 dynamic_slice.51
  307.6 0.7 fusion.62
  308.9 0.7 fusion.63
  310.3 15.8 %gather_fusion.2 = bf16[144,128,128]{2,1,0:T(8,128)(2,1)} fusion(bf16[24,12,128,128]{3,2,1,0:T(8,128)(2,1)} %get-tuple-element.305, s32[144]{0:T(256)S(1)} %reshape.191), kind=kCustom, calls=%fused_computation.1.clone.clone.1 | custom fusion | bytes 9438336 | tf_op jit(solution)/shard_map/while/body/eval_jaxpr/gather | solution.py:45
  326.1 6.7 %copy.17 = bf16[12,12,128,128]{2,3,1,0:T(8,128)(2,1)} copy(bf16[12,12,128,128]{3,2,1,0:T(8,128)(2,1)} %bitcast.95) | data formatting | bytes 9437184 | tf_op jit(solution)/shard_map/while/body/eval_jaxpr/gather | solution.py:45
  333.4 4.8 fusion.66
  338.2 0.6 dynamic_slice.51
  341.3 0.7 fusion.62
  342.6 0.7 fusion.63
  344.0 15.8 %gather_fusion.2 = bf16[144,128,128]{2,1,0:T(8,128)(2,1)} fusion(bf16[24,12,128,128]{3,2,1,0:T(8,128)(2,1)} %get-tuple-element.305, s32[144]{0:T(256)S(1)} %reshape.191), kind=kCustom, calls=%fused_computation.1.clone.clone.1 | custom fusion | bytes 9438336 | tf_op jit(solution)/shard_map/while/body/eval_jaxpr/gather | solution.py:45
  359.8 6.7 %copy.17 = bf16[12,12,128,128]{2,3,1,0:T(8,128)(2,1)} copy(bf16[12,12,128,128]{3,2,1,0:T(8,128)(2,1)} %bitcast.95) | data formatting | bytes 9437184 | tf_op jit(solution)/shard_map/while/body/eval_jaxpr/gather | solution.py:45
  367.1 4.8 fusion.66
  371.9 1.9 convolution_bitcast_fusion
  373.8 269.0 %all-reduce.2.cloned.1.call-done = f32[128,128]{0,1:T(8,128)} async-done(((f32[128,128]{0,1:T(8,128)}), f32[128,128]{0,1:T(8,128)}) %all-reduce.2.cloned.1.call-update) | async-done | bytes 65552 | tf_op jit(solution)/shard_map/psum | solution.py:56
  642.8 0.8 broadcast_multiply_fusion
  643.6 0.7 copy.13
  (70 shorter events, 13.5 us)
Async XLA Ops:
  7.2 635.6 %all-reduce.2.cloned.1.call-start = ((), (), s32[]{:S(2)}) async-start(), calls=%async_computation | async-start | bytes 131072 | tf_op jit(solution)/shard_map/psum | solution.py:56
  7.2 87.3 %collective-permute-start = (bf16[8,12,128,128]{3,2,1,0:T(8,128)(2,1)}, bf16[8,12,128,128]{3,2,1,0:T(8,128)(2,1)}, u32[]{:S(2)}, u32[]{:S(2)}) collective-permute-start(bf16[8,12,128,128]{3,2,1,0:T(8,128)(2,1)} %param.6), channel_id=1, source_target_pairs={{0,1},{1,2},{2,3},{3,4},{4,5},{5,6},{6,7},{7,8},{8,9},{9,10},{10,1... | collective-permute-start | bytes 9437192 | tf_op jit(solution)/shard_map/ppermute | solution.py:14
  14.4 80.1 %collective-permute-start.1 = (bf16[8,12,128,128]{3,2,1,0:T(8,128)(2,1)}, bf16[8,12,128,128]{3,2,1,0:T(8,128)(2,1)}, u32[]{:S(2)}, u32[]{:S(2)}) collective-permute-start(bf16[8,12,128,128]{3,2,1,0:T(8,128)(2,1)} %param.6), channel_id=1, source_target_pairs={{1,0},{2,1},{3,2},{4,3},{5,4},{6,5},{7,6},{8,7},{9,8},{10,9},{11,1... | collective-permute-start | bytes 9437192 | tf_op jit(solution)/shard_map/ppermute | solution.py:16
  17.9 69.6 %collective-permute-start.2 = (bf16[1024,128]{1,0:T(8,128)(2,1)}, bf16[1024,128]{1,0:T(8,128)(2,1)S(1)}, u32[]{:S(2)}, u32[]{:S(2)}) collective-permute-start(bf16[1024,128]{1,0:T(8,128)(2,1)} %param.9), channel_id=1, source_target_pairs={{0,1},{1,2},{2,3},{3,4},{4,5},{5,6},{6,7},{7,8},{8,9},{9,10},{10,1... | collective-permute-start | bytes 786440 | tf_op jit(solution)/shard_map/ppermute | solution.py:14
  20.9 72.6 %collective-permute-start.3 = (bf16[1024,128]{1,0:T(8,128)(2,1)}, bf16[1024,128]{1,0:T(8,128)(2,1)S(1)}, u32[]{:S(2)}, u32[]{:S(2)}) collective-permute-start(bf16[1024,128]{1,0:T(8,128)(2,1)} %param.9), channel_id=1, source_target_pairs={{1,0},{2,1},{3,2},{4,3},{5,4},{6,5},{7,6},{8,7},{9,8},{10,9},{11,1... | collective-permute-start | bytes 786440 | tf_op jit(solution)/shard_map/ppermute | solution.py:16
  102.2 269.7 %copy-start = (bf16[1024,128]{1,0:T(8,128)(2,1)S(1)}, bf16[1024,128]{1,0:T(8,128)(2,1)}, u32[]{:S(2)}) copy-start(bf16[1024,128]{1,0:T(8,128)(2,1)} %param.9) | copy-start | bytes 786436
Sparse Core Ops, SparseCore 0:
  373.9 268.8 all-reduce.1
where the time goes:
time: 654 us; the launch traced here: 651 us
  waiting for transfers between devices  331 us (51%)
  local copies, waits for them, and re-layouts  198 us (30%)
  matrix products  40 us (6%)
  other arithmetic  25.5 us (4%)
  starting transfers between devices  22.8 us (3%)
  loops' own time  20.3 us (3%)
  between operations  14.1 us (2%)
    psum x1, waiting for transfers between devices, per_device(): level = lax.psum(partial_level, ('wide', 'narrow'))  269 us
    gather x16, local copies, waits for them, and re-layouts, one_row(): chosen = extended[places[None, :], which]  180 us
    ppermute x2, waiting for transfers between devices, with_halo(): lax.ppermute(tail, axis, [(i, (i + 1) % count) for i in range(count)])  55.9 us
    dot_general x8, matrix products, one_row(): jnp.einsum('oac,ock->ak', square, picked, preferred_element_type=jnp.floa...  38.2 us
    another operation x1, loops' own time, per_device(): lax.map(one_row, jnp.arange(local, dtype=jnp.int32))  20.3 us
  transfers between devices with their start and end apart: 5, of which 3 were waited for; matrix products, arithmetic and copies ran while one was open for 0% of the time, Pallas kernels for 0%

commit v1 on v0

v1 whole, which is shorter than its diff:
```python
import jax
import jax.numpy as jnp
from jax import lax
from jax.experimental import pallas as pl
from jax.experimental.pallas import tpu as pltpu
from jax.sharding import Mesh
from jax.sharding import PartitionSpec as P

LOCAL = 8
B = 128
SLOTS = 12
PAIRS = 36
RANKS = ("y", "x", "zl", "zh", "core")
RING = ("zl", "zh", "core")
PLANE = ("y", "x")


def right_place(r, j):
    return r * (r + 1) // 2 + j


def left_place(r, j):
    return LOCAL * r - r * (r - 1) // 2 + j - r


def pack_kernel(tcol, tval, to_right, to_left, table, sems):
    for p in range(2 * PAIRS):
        table[p] = 0
    for r in range(LOCAL):
        for s in range(SLOTS):
            v = tcol[LOCAL + r, s]
            place = jnp.where(
                v >= 2 * LOCAL,
                r * (r + 1) // 2 + v - 2 * LOCAL,
                jnp.where(v < LOCAL, PAIRS + LOCAL * r - r * (r - 1) // 2 + v - r, 2 * PAIRS),
            )
            table[place] = s
    copies = []
    for r in range(LOCAL):
        for j in range(LOCAL):
            if j <= r:
                p = right_place(r, j)
                copies.append(
                    pltpu.make_async_copy(tval.at[r, table[p]], to_right.at[:, pl.ds(p * B, B)], sems.at[p])
                )
                copies[-1].start()
            if j >= r:
                p = left_place(r, j)
                copies.append(
                    pltpu.make_async_copy(
                        tval.at[r, table[PAIRS + p]], to_left.at[:, pl.ds(p * B, B)], sems.at[PAIRS + p]
                    )
                )
                copies[-1].start()
    for copy in copies:
        copy.wait()


def pack(tcol, tval):
    out = jax.ShapeDtypeStruct((B, PAIRS * B), jnp.bfloat16)
    return pl.pallas_call(
        pack_kernel,
        out_shape=(out, out),
        in_specs=[pl.BlockSpec(memory_space=pltpu.SMEM), pl.BlockSpec(memory_space=pl.ANY)],
        out_specs=(pl.BlockSpec(memory_space=pl.ANY), pl.BlockSpec(memory_space=pl.ANY)),
        scratch_shapes=[pltpu.SMEM((2 * PAIRS + 1,), jnp.int32), pltpu.SemaphoreType.DMA((2 * PAIRS,))],
        name="pack",
    )(tcol, tval)


def inner_kernel(tcol, wanted, held, tval, basis_l, basis, basis_r, y_out, p_out, level, basis_t, blocks, z, y_own):
    for part, ref in enumerate((basis_l, basis, basis_r)):
        blocks[part * LOCAL * B : (part + 1) * LOCAL * B, :] = ref[: LOCAL * B, :]
    y_own[LOCAL * LOCAL * B :, :] = jnp.zeros((B, B), jnp.bfloat16)

    @pl.loop(0, LOCAL)
    def _(j):
        for s in range(SLOTS):
            c = tcol[LOCAL + j, s]
            z[s] = jnp.dot(
                tval[j, s],
                blocks[pl.ds(pl.multiple_of(c * B, B), B), :],
                preferred_element_type=jnp.float32,
            )

        @pl.loop(0, 2 * LOCAL + 1)
        def _(d):
            i = j + d
            r = i & (LOCAL - 1)
            part = i >> 3
            own = part == 1
            place = jnp.where(part == 0, (r * (r + 1) >> 1) + j, PAIRS + LOCAL * r - (r * (r - 1) >> 1) + j - r)
            place = jnp.where(own, r * LOCAL + j, place)
            rows = pl.ds(pl.multiple_of(place * B, B), B)
            on = held[i, j]

            def total():
                y = jnp.zeros((B, B), jnp.float32)
                for s in range(SLOTS):
                    y = y + wanted[i, tcol[LOCAL + j, s]] * z[s]
                return y.astype(jnp.bfloat16)

            @pl.when(jnp.logical_and(own, on == 1))
            def _():
                y_own[rows, :] = total()

            @pl.when(jnp.logical_and(jnp.logical_not(own), on == 1))
            def _():
                y_out[rows, :] = total()

            @pl.when(jnp.logical_and(jnp.logical_not(own), on == 0))
            def _():
                y_out[rows, :] = jnp.zeros((B, B), jnp.bfloat16)

    level[...] = jnp.zeros((B, B), jnp.float32)

    @pl.loop(0, LOCAL)
    def _(r):
        p = jnp.zeros((B, B), jnp.float32)
        for s in range(SLOTS):
            v = tcol[LOCAL + r, s] - LOCAL
            inside = jnp.logical_and(v >= 0, v < LOCAL)
            place = jnp.where(inside, r * LOCAL + v, LOCAL * LOCAL)
            p = p + jnp.dot(
                tval[r, s],
                y_own[pl.ds(pl.multiple_of(place * B, B), B), :],
                preferred_element_type=jnp.float32,
            )
        rows = pl.ds(pl.multiple_of(r * B, B), B)
        p_out[rows, :] = p
        level[...] += lax.dot_general(
            basis[rows, :], p.astype(jnp.bfloat16), (((0,), (0,)), ((), ())), preferred_element_type=jnp.float32
        )

    for part, ref in enumerate((basis_l, basis_r)):
        for r in range(LOCAL):
            place = (part * LOCAL + r) * B
            basis_t[:, place : place + B] = ref[r * B : (r + 1) * B, :].T


def inner(tcol, wanted, held, tval, basis_l, basis, basis_r):
    vmem = pl.BlockSpec(memory_space=pltpu.VMEM)
    smem = pl.BlockSpec(memory_space=pltpu.SMEM)
    return pl.pallas_call(
        inner_kernel,
        out_shape=(
            jax.ShapeDtypeStruct((2 * PAIRS * B, B), jnp.bfloat16),
            jax.ShapeDtypeStruct((LOCAL * B, B), jnp.float32),
            jax.ShapeDtypeStruct((B, B), jnp.float32),
            jax.ShapeDtypeStruct((B, 2 * LOCAL * B), jnp.bfloat16),
        ),
        in_specs=[smem, smem, smem, vmem, vmem, vmem, vmem],
        out_specs=(vmem, vmem, vmem, vmem),
        scratch_shapes=[
            pltpu.VMEM((3 * LOCAL * B, B), jnp.bfloat16),
            pltpu.VMEM((SLOTS, B, B), jnp.float32),
            pltpu.VMEM(((LOCAL * LOCAL + 1) * B, B), jnp.bfloat16),
        ],
        compiler_params=pltpu.CompilerParams(vmem_limit_bytes=28 * 1024 * 1024),
        cost_estimate=pl.CostEstimate(flops=12_000_000_000, bytes_accessed=8_000_000, transcendentals=0),
        name="inner",
    )(tcol, wanted, held, tval, basis_l, basis, basis_r)


def outer_kernel(from_left, from_right, y, basis_t, level_in, p_left, p_right, level):
    total = level_in[...]
    for r in range(LOCAL):
        at = right_place(r, 0) * B
        span = (r + 1) * B
        p = jnp.dot(from_left[:, at : at + span], y[at : at + span, :], preferred_element_type=jnp.float32)
        p_left[r * B : (r + 1) * B, :] = p.astype(jnp.bfloat16)
    for r in range(LOCAL):
        at = left_place(r, r) * B
        span = (LOCAL - r) * B
        p = jnp.dot(
            from_right[:, at : at + span],
            y[PAIRS * B + at : PAIRS * B + at + span, :],
            preferred_element_type=jnp.float32,
        )
        p_right[r * B : (r + 1) * B, :] = p.astype(jnp.bfloat16)
    total += jnp.dot(basis_t[:, : LOCAL * B], p_left[...], preferred_element_type=jnp.float32)
    total += jnp.dot(basis_t[:, LOCAL * B :], p_right[...], preferred_element_type=jnp.float32)
    level[...] = total


def outer(from_left, from_right, y, basis_t, level):
    vmem = pl.BlockSpec(memory_space=pltpu.VMEM)
    rows = jax.ShapeDtypeStruct((LOCAL * B, B), jnp.bfloat16)
    return pl.pallas_call(
        outer_kernel,
        out_shape=(rows, rows, jax.ShapeDtypeStruct((B, B), jnp.float32)),
        in_specs=[vmem] * 5,
        out_specs=(vmem, vmem, vmem),
        compiler_params=pltpu.CompilerParams(vmem_limit_bytes=20 * 1024 * 1024),
        name="outer",
    )(from_left, from_right, y, basis_t, level)


def copies(part, count):
    return jnp.broadcast_to(part[None], (count,) + part.shape)


def per_device(tval, tcol, ocol, basis):
    devices = lax.axis_size(RANKS)
    count = LOCAL * devices
    me = lax.axis_index(RANKS)
    first = me * LOCAL
    onward = [(i, (i + 1) % devices) for i in range(devices)]
    back = [((i + 1) % devices, i) for i in range(devices)]

    ring = lax.axis_size(RING)
    plane = lax.axis_size(PLANE)

    places = (ocol - first + 2 * LOCAL + count) % count
    mine = jnp.any(places[:, :, None] == jnp.arange(B, dtype=jnp.int32), axis=1).astype(jnp.bfloat16)
    sent = jnp.concatenate([basis, mine, jnp.zeros_like(mine)], axis=0)
    basis_l = lax.ppermute(sent, RANKS, onward)
    basis_r = lax.ppermute(sent, RANKS, back)

    near = jnp.concatenate(
        [lax.dynamic_slice_in_dim(tcol, ((me + k) % devices) * LOCAL, LOCAL, 0) for k in (devices - 1, 0, 1)]
    )
    near = (near - first + LOCAL + count) % count
    held = jnp.any(near[:, :, None] == LOCAL + jnp.arange(LOCAL, dtype=jnp.int32), axis=1).astype(jnp.int32)
    to_right, to_left = pack(near, tval)
    from_left = lax.ppermute(to_right, RANKS, onward)
    from_right = lax.ppermute(to_left, RANKS, back)

    rows = LOCAL * B
    wanted = jnp.concatenate(
        [
            basis_l[rows : rows + LOCAL, 2 * LOCAL : 5 * LOCAL],
            mine[:, LOCAL : 4 * LOCAL],
            basis_r[rows : rows + LOCAL, : 3 * LOCAL],
        ]
    ).astype(jnp.float32)
    y, p_own, level, basis_t = inner(near, wanted, held, tval, basis_l, basis, basis_r)
    p_left, p_right, level = outer(from_left, from_right, y, basis_t, level)

    theirs_r = lax.ppermute(p_left, RANKS, back)
    theirs_l = lax.ppermute(p_right, RANKS, onward)

    level = lax.all_to_all(level.reshape(ring, B // ring, B), RING, 0, 0).sum(0)
    level = lax.all_to_all(copies(level, plane), PLANE, 0, 0).sum(0)
    level = level / jnp.sqrt(jnp.float32(count * B))
    level = lax.all_to_all(copies(level, ring), RING, 0, 0).reshape(B, B)

    projected = p_own + theirs_l.astype(jnp.float32) + theirs_r.astype(jnp.float32)
    return (projected.astype(jnp.bfloat16), level)


def solution(mesh):
    mesh = Mesh(mesh.devices.reshape(8, 4, 2, 4, 2), RANKS)
    return jax.shard_map(
        per_device,
        mesh=mesh,
        in_specs=(P(RANKS, None, None, None), P(), P(RANKS, None), P(RANKS, None)),
        out_specs=(P(RANKS, None), P()),
        check_vma=False,
    )
```

time: 654 us -> 179 us (0.27)
  waiting for transfers between devices: 331 us -> 12.9 us
  local copies, waits for them, and re-layouts: 198 us -> 5.61 us
  Pallas kernels: 0 us -> 96 us
  matrix products: 40 us -> 0 us
  other arithmetic: 25.5 us -> 4.24 us
  loops' own time: 20.3 us -> 0 us
  starting transfers between devices: 22.8 us -> 41.3 us
  blocking collectives: 0 us -> 17.7 us
  between operations: 14.1 us -> 0.88 us
    psum x1 -> x0, waiting for transfers between devices: 269 us -> none  [per_device(): level = lax.psum(partial_level, ('wide', 'narrow'))]
    gather x32 -> x0, local copies, waits for them, and re-layouts: 189 us -> none  [the longest x16 180 us: one_row(): chosen = extended[places[None, :], which]]
    pallas_call x0 -> x3, Pallas kernels: none -> 96 us  [the longest x1 74.5 us: pack(): pl.pallas_call(pack_kernel, out_shape=(out, out), in_specs=[pl.BlockSpec(...]
    ppermute x4 -> x6, waiting for transfers between devices: 61.9 us -> 1.11 us  [the longest x1 1.1 us: per_device(): from_right = lax.ppermute(to_left, RANKS, back)]
    dot_general x9 -> x0, matrix products: 40 us -> none  [the longest x8 38.2 us: one_row(): jnp.einsum('oac,ock->ak', square, picked, preferred_element_type=jnp.floa...]
    another operation x1 -> x0, loops' own time: 20.3 us -> none  [per_device(): lax.map(one_row, jnp.arange(local, dtype=jnp.int32))]
    all_to_all x0 -> x1, blocking collectives: none -> 17.7 us  [per_device(): level = lax.all_to_all(level.reshape(ring, B // ring, B), RING, 0, 0).sum(0)]
    all_to_all x0 -> x2, starting transfers between devices: none -> 13.9 us  [the longest x1 8.54 us: per_device(): level = lax.all_to_all(copies(level, plane), PLANE, 0, 0).sum(0)]
  transfers between devices with their start and end apart: 5 -> 8, of which waited for: 3 -> 3; matrix products, arithmetic and copies ran while one was open for 0% -> 3% of each run, Pallas kernels for 0% -> 52%
where the time goes in v1:
time: 179 us
  Pallas kernels  96 us (54%)
  starting transfers between devices  41.3 us (23%)
  blocking collectives  17.7 us (10%)
  waiting for transfers between devices  12.9 us (7%)
  local copies, waits for them, and re-layouts  5.61 us (3%)
  other arithmetic  4.24 us (2%)
    pallas_call x1, Pallas kernels, pack(): pl.pallas_call(pack_kernel, out_shape=(out, out), in_specs=[pl.BlockSpec(...  74.5 us
    pallas_call x1, Pallas kernels, inner(): pl.pallas_call(inner_kernel, out_shape=(jax.ShapeDtypeStruct((2 * PAIRS *...  19 us
    all_to_all x1, blocking collectives, per_device(): level = lax.all_to_all(level.reshape(ring, B // ring, B), RING, 0, 0).sum(0)  17.7 us
    ppermute x1, starting transfers between devices, per_device(): from_right = lax.ppermute(to_left, RANKS, back)  10.1 us
    ppermute x1, starting transfers between devices, per_device(): basis_r = lax.ppermute(sent, RANKS, back)  8.78 us
    all_to_all x1, starting transfers between devices, per_device(): level = lax.all_to_all(copies(level, plane), PLANE, 0, 0).sum(0)  8.54 us
    all_to_all x1, waiting for transfers between devices, per_device(): level = lax.all_to_all(copies(level, ring), RING, 0, 0).reshape(B, B)  7 us
    all_to_all x1, starting transfers between devices, per_device(): level = lax.all_to_all(copies(level, ring), RING, 0, 0).reshape(B, B)  5.4 us
  transfers between devices with their start and end apart: 8, of which 3 were waited for; matrix products, arithmetic and copies ran while one was open for 3% of the time, Pallas kernels for 52%

profile of v1, /device:TPU:1, one launch (start us, length us, event | category | flops | bytes accessed | tf_op | source)
XLA Modules:
  0.0 178.6 jit_solution(2076464050525226534)
XLA Ops:
  0.6 0.7 add_select_fusion.1
  1.3 0.1 copy.18
  1.4 0.1 fusion
  1.5 0.1 pad.5.clone
  1.6 1.9 %maximum_maximum_fusion = bf16[1040,128]{1,0:T(8,128)(2,1)} fusion(bf16[8,128]{1,0:T(8,128)(2,1)S(1)} %convert_element_type.18, bf16[1024,128]{1,0:T(8,128)(2,1)} %basis.1, bf16[1040]{0:T(1024)(128)(2,1)S(1)} %pad.5.clone), kind=kLoop, calls=%fused_computation.1 | loop fusion | flops 798720 | bytes 532512 | tf_op jit(solution)/shard_map/concatenate | solution.py:216
  3.5 8.8 %collective-permute-start.1 = (bf16[1040,128]{1,0:T(8,128)(2,1)}, bf16[1040,128]{1,0:T(8,128)(2,1)}, u32[]{:S(2)}, u32[]{:S(2)}) collective-permute-start(bf16[1040,128]{1,0:T(8,128)(2,1)} %maximum_maximum_fusion), channel_id=1, source_target_pairs={{1,0},{2,1},{3,2},{4,3},{5,4},{6,5},{7,6},{8,7},{9,8},{10,9},{11,1... | collective-permute-start | bytes 798728 | tf_op jit(solution)/shard_map/ppermute | solution.py:218
  12.3 1.9 %collective-permute-start = (bf16[1040,128]{1,0:T(8,128)(2,1)}, bf16[1040,128]{1,0:T(8,128)(2,1)}, u32[]{:S(2)}, u32[]{:S(2)}) collective-permute-start(bf16[1040,128]{1,0:T(8,128)(2,1)} %maximum_maximum_fusion), channel_id=1, source_target_pairs={{0,1},{1,2},{2,3},{3,4},{4,5},{5,6},{6,7},{7,8},{8,9},{9,10},{10,1... | collective-permute-start | bytes 798728 | tf_op jit(solution)/shard_map/ppermute | solution.py:217
  14.2 0.0 copy-start.3
  14.3 0.9 constant_dynamic-slice_fusion.2
  15.2 0.1 copy.21
  15.2 0.1 copy.22
  15.3 0.1 copy.23
  15.4 0.6 add_select_fusion.tcol
  16.0 0.0 copy-start
  16.0 0.0 copy-start.4
  16.0 74.5 %pack.1 = (bf16[128,4608]{1,0:T(8,128)(2,1)}, bf16[128,4608]{1,0:T(8,128)(2,1)}) custom-call(s32[24,12]{1,0:T(8,128)} %add_select_fusion.tcol, bf16[8,12,128,128]{3,2,1,0:T(8,128)(2,1)} %tval.3), custom_call_target="tpu_custom_call" | custom-call | tf_op jit(solution)/shard_map/pack/pallas_call | solution.py:61
  90.5 1.9 %collective-permute-start.2 = (bf16[128,4608]{1,0:T(8,128)(2,1)}, bf16[128,4608]{1,0:T(8,128)(2,1)}, u32[]{:S(2)}, u32[]{:S(2)}) collective-permute-start(bf16[128,4608]{1,0:T(8,128)(2,1)} %get-tuple-element.12), channel_id=1, source_target_pairs={{0,1},{1,2},{2,3},{3,4},{4,5},{5,6},{6,7},{7,8},{8,9},{9,10},{10,1... | collective-permute-start | bytes 3538952 | tf_op jit(solution)/shard_map/ppermute | solution.py:226
  92.4 10.1 %collective-permute-start.3 = (bf16[128,4608]{1,0:T(8,128)(2,1)}, bf16[128,4608]{1,0:T(8,128)(2,1)}, u32[]{:S(2)}, u32[]{:S(2)}) collective-permute-start(bf16[128,4608]{1,0:T(8,128)(2,1)} %get-tuple-element.13), channel_id=1, source_target_pairs={{1,0},{2,1},{3,2},{4,3},{5,4},{6,5},{7,6},{8,7},{9,8},{10,9},{11,1... | collective-permute-start | bytes 3538952 | tf_op jit(solution)/shard_map/ppermute | solution.py:227
  102.5 0.1 slice.10
  102.6 0.8 copy.19
  103.4 0.1 compare_reduce_fusion
  103.5 0.1 copy.20.held
  103.5 0.0 collective-permute-done.1.basis_r
  103.5 0.7 slice.13
  104.2 0.0 collective-permute-done.basis_l
  104.2 0.7 slice.12
  105.0 0.0 copy-done.3
  105.0 0.0 copy-done
  105.0 0.0 copy-done.4
  105.0 19.0 %inner.1 = (bf16[9216,128]{1,0:T(8,128)(2,1)S(1)}, f32[1024,128]{1,0:T(8,128)S(1)}, f32[128,128]{1,0:T(8,128)S(1)}, bf16[128,2048]{1,0:T(8,128)(2,1)S(1)}) custom-call(s32[24,12]{1,0:T(8,128)S(1)} %copy-done.4, f32[24,24]{1,0:T(8,128)S(1)} %maximum_convert_fusion.wanted, s32[24,8]{1,0:T(8,128)S(1)} %copy.20.held, bf16[8,12,128,128]{3,2,1,0:T(8,128)(2,1)S(1)} %copy-done, ...), custom_call_target="tpu_custom_call" | custom-call | flops 12000000000 | bytes 8000000 | tf_op jit(solution)/shard_map/inner/pallas_call | solution.py:144
  124.0 0.0 copy-start.1
  124.0 0.0 collective-permute-done.2.from_left
  124.0 1.1 collective-permute-done.3.from_right
  125.1 2.6 %outer.1 = (bf16[1024,128]{1,0:T(8,128)(2,1)S(1)}, bf16[1024,128]{1,0:T(8,128)(2,1)S(1)}, f32[128,128]{1,0:T(8,128)S(1)}) custom-call(bf16[128,4608]{1,0:T(8,128)(2,1)} %collective-permute-done.2.from_left, bf16[128,4608]{1,0:T(8,128)(2,1)} %collective-permute-done.3.from_right, bf16[9216,128]{1,0:T(8,128)(2,1)S(1)} %get-tuple-element.14.y, ...), custom_call_target="tpu_custom_call" | custom-call | tf_op jit(solution)/shard_map/outer/pallas_call | solution.py:189
  127.7 0.0 copy-done.1
  127.7 0.0 copy-start.2
  127.7 17.7 %all_to_all.15 = f32[16,8,128]{2,1,0:T(8,128)S(1)} all-to-all(f32[16,8,128]{2,1,0:T(8,128)S(1)} %bitcast.2), channel_id=1, replica_groups=mesh['y'=8,'x'=4,'zl'=2,'zh'=4,'core'=2] {'zl','zh','core'}, dimensions={0} | all-to-all | bytes 131072 | tf_op jit(solution)/shard_map/all_to_all | solution.py:243
  145.4 0.7 broadcast_in_dim.7
  146.1 8.5 %all-to-all-start.1 = ((f32[32,8,128]{2,1,0:T(8,128)}), f32[32,8,128]{2,1,0:T(8,128)S(1)}, u32[]{:S(2)}, u32[]{:S(2)}) async-start(f32[32,8,128]{2,1,0:T(8,128)} %broadcast_in_dim.7), calls=%async_computation.1 | async-start | bytes 262144 | tf_op jit(solution)/shard_map/all_to_all | solution.py:244
  154.6 2.7 %collective-permute-start.4 = (bf16[1024,128]{1,0:T(8,128)(2,1)S(1)}, bf16[1024,128]{1,0:T(8,128)(2,1)S(1)}, u32[]{:S(2)}, u32[]{:S(2)}) collective-permute-start(bf16[1024,128]{1,0:T(8,128)(2,1)S(1)} %get-tuple-element.17), channel_id=1, source_target_pairs={{0,1},{1,2},{2,3},{3,4},{4,5},{5,6},{6,7},{7,8},{8,9},{9,10},{10,1... | collective-permute-start | bytes 786440 | tf_op jit(solution)/shard_map/ppermute | solution.py:241
  157.4 1.9 %collective-permute-start.5 = (bf16[1024,128]{1,0:T(8,128)(2,1)S(1)}, bf16[1024,128]{1,0:T(8,128)(2,1)S(1)}, u32[]{:S(2)}, u32[]{:S(2)}) collective-permute-start(bf16[1024,128]{1,0:T(8,128)(2,1)S(1)} %get-tuple-element.18), channel_id=1, source_target_pairs={{1,0},{2,1},{3,2},{4,3},{5,4},{6,5},{7,6},{8,7},{9,8},{10,9},{11,1... | collective-permute-start | bytes 786440 | tf_op jit(solution)/shard_map/ppermute | solution.py:240
  159.3 4.8 %all-to-all-done.1 = f32[32,8,128]{2,1,0:T(8,128)S(1)} async-done(((f32[32,8,128]{2,1,0:T(8,128)}), f32[32,8,128]{2,1,0:T(8,128)S(1)}, u32[]{:S(2)}, u32[]{:S(2)}) %all-to-all-start.1) | async-done | bytes 131104 | tf_op jit(solution)/shard_map/all_to_all | solution.py:244
  164.1 0.6 broadcast_in_dim.8
  164.8 5.4 %all-to-all-start.2 = ((f32[16,8,128]{2,1,0:T(8,128)}), f32[16,8,128]{2,1,0:T(8,128)S(1)}, u32[]{:S(2)}, u32[]{:S(2)}) async-start(f32[16,8,128]{2,1,0:T(8,128)} %broadcast_in_dim.8), calls=%async_computation.2 | async-start | bytes 131072 | tf_op jit(solution)/shard_map/all_to_all | solution.py:246
  170.2 0.0 collective-permute-done.4
  170.2 0.0 collective-permute-done.5
  170.2 0.0 copy-done.2
  170.2 0.8 add_convert_fusion
  171.0 7.0 %all-to-all-done.2 = f32[16,8,128]{2,1,0:T(8,128)S(1)} async-done(((f32[16,8,128]{2,1,0:T(8,128)}), f32[16,8,128]{2,1,0:T(8,128)S(1)}, u32[]{:S(2)}, u32[]{:S(2)}) %all-to-all-start.2) | async-done | bytes 65568 | tf_op jit(solution)/shard_map/all_to_all | solution.py:246
  178.0 0.6 copy.25
  (8 shorter events, 0.1 us)
Async XLA Ops:
  3.5 100.0 %collective-permute-start.1 = (bf16[1040,128]{1,0:T(8,128)(2,1)}, bf16[1040,128]{1,0:T(8,128)(2,1)}, u32[]{:S(2)}, u32[]{:S(2)}) collective-permute-start(bf16[1040,128]{1,0:T(8,128)(2,1)} %maximum_maximum_fusion), channel_id=1, source_target_pairs={{1,0},{2,1},{3,2},{4,3},{5,4},{6,5},{7,6},{8,7},{9,8},{10,9},{11,1... | collective-permute-start | bytes 798728 | tf_op jit(solution)/shard_map/ppermute | solution.py:218
  12.3 92.0 %collective-permute-start = (bf16[1040,128]{1,0:T(8,128)(2,1)}, bf16[1040,128]{1,0:T(8,128)(2,1)}, u32[]{:S(2)}, u32[]{:S(2)}) collective-permute-start(bf16[1040,128]{1,0:T(8,128)(2,1)} %maximum_maximum_fusion), channel_id=1, source_target_pairs={{0,1},{1,2},{2,3},{3,4},{4,5},{5,6},{6,7},{7,8},{8,9},{9,10},{10,1... | collective-permute-start | bytes 798728 | tf_op jit(solution)/shard_map/ppermute | solution.py:217
  14.2 90.8 %copy-start.3 = (bf16[1024,128]{1,0:T(8,128)(2,1)S(1)}, bf16[1024,128]{1,0:T(8,128)(2,1)}, u32[]{:S(2)}) copy-start(bf16[1024,128]{1,0:T(8,128)(2,1)} %basis.1) | copy-start | bytes 786436
  16.0 89.0 %copy-start = (bf16[8,12,128,128]{3,2,1,0:T(8,128)(2,1)S(1)}, bf16[8,12,128,128]{3,2,1,0:T(8,128)(2,1)}, u32[]{:S(2)}) copy-start(bf16[8,12,128,128]{3,2,1,0:T(8,128)(2,1)} %tval.3) | copy-start | bytes 9437188
  16.0 89.0 %copy-start.4 = (s32[24,12]{1,0:T(8,128)S(1)}, s32[24,12]{1,0:T(8,128)}, u32[]{:S(2)}) copy-start(s32[24,12]{1,0:T(8,128)} %add_select_fusion.tcol) | copy-start | bytes 3460
  90.5 33.5 %collective-permute-start.2 = (bf16[128,4608]{1,0:T(8,128)(2,1)}, bf16[128,4608]{1,0:T(8,128)(2,1)}, u32[]{:S(2)}, u32[]{:S(2)}) collective-permute-start(bf16[128,4608]{1,0:T(8,128)(2,1)} %get-tuple-element.12), channel_id=1, source_target_pairs={{0,1},{1,2},{2,3},{3,4},{4,5},{5,6},{6,7},{7,8},{8,9},{9,10},{10,1... | collective-permute-start | bytes 3538952 | tf_op jit(solution)/shard_map/ppermute | solution.py:226
  92.4 32.7 %collective-permute-start.3 = (bf16[128,4608]{1,0:T(8,128)(2,1)}, bf16[128,4608]{1,0:T(8,128)(2,1)}, u32[]{:S(2)}, u32[]{:S(2)}) collective-permute-start(bf16[128,4608]{1,0:T(8,128)(2,1)} %get-tuple-element.13), channel_id=1, source_target_pairs={{1,0},{2,1},{3,2},{4,3},{5,4},{6,5},{7,6},{8,7},{9,8},{10,9},{11,1... | collective-permute-start | bytes 3538952 | tf_op jit(solution)/shard_map/ppermute | solution.py:227
  124.0 3.7 %copy-start.1 = (f32[1024,128]{1,0:T(8,128)}, f32[1024,128]{1,0:T(8,128)S(1)}, u32[]{:S(2)}) copy-start(f32[1024,128]{1,0:T(8,128)S(1)} %get-tuple-element.11) | copy-start | bytes 1572868
  127.7 42.5 %copy-start.2 = (f32[1024,128]{1,0:T(8,128)S(1)}, f32[1024,128]{1,0:T(8,128)}, u32[]{:S(2)}) copy-start(f32[1024,128]{1,0:T(8,128)} %copy-done.1) | copy-start | bytes 1572868
  146.1 18.0 %all-to-all-start.1 = ((f32[32,8,128]{2,1,0:T(8,128)}), f32[32,8,128]{2,1,0:T(8,128)S(1)}, u32[]{:S(2)}, u32[]{:S(2)}) async-start(f32[32,8,128]{2,1,0:T(8,128)} %broadcast_in_dim.7), calls=%async_computation.1 | async-start | bytes 262144 | tf_op jit(solution)/shard_map/all_to_all | solution.py:244
  154.6 15.5 %collective-permute-start.4 = (bf16[1024,128]{1,0:T(8,128)(2,1)S(1)}, bf16[1024,128]{1,0:T(8,128)(2,1)S(1)}, u32[]{:S(2)}, u32[]{:S(2)}) collective-permute-start(bf16[1024,128]{1,0:T(8,128)(2,1)S(1)} %get-tuple-element.17), channel_id=1, source_target_pairs={{0,1},{1,2},{2,3},{3,4},{4,5},{5,6},{6,7},{7,8},{8,9},{9,10},{10,1... | collective-permute-start | bytes 786440 | tf_op jit(solution)/shard_map/ppermute | solution.py:241
  157.4 12.8 %collective-permute-start.5 = (bf16[1024,128]{1,0:T(8,128)(2,1)S(1)}, bf16[1024,128]{1,0:T(8,128)(2,1)S(1)}, u32[]{:S(2)}, u32[]{:S(2)}) collective-permute-start(bf16[1024,128]{1,0:T(8,128)(2,1)S(1)} %get-tuple-element.18), channel_id=1, source_target_pairs={{1,0},{2,1},{3,2},{4,3},{5,4},{6,5},{7,6},{8,7},{9,8},{10,9},{11,1... | collective-permute-start | bytes 786440 | tf_op jit(solution)/shard_map/ppermute | solution.py:240
  164.8 13.2 %all-to-all-start.2 = ((f32[16,8,128]{2,1,0:T(8,128)}), f32[16,8,128]{2,1,0:T(8,128)S(1)}, u32[]{:S(2)}, u32[]{:S(2)}) async-start(f32[16,8,128]{2,1,0:T(8,128)} %broadcast_in_dim.8), calls=%async_computation.2 | async-start | bytes 131072 | tf_op jit(solution)/shard_map/all_to_all | solution.py:246

commit v2 on v1

v2 whole, which is shorter than its diff:
```python
import functools

import jax
import jax.numpy as jnp
from jax import lax
from jax.experimental import pallas as pl
from jax.experimental.pallas import tpu as pltpu
from jax.sharding import Mesh
from jax.sharding import PartitionSpec as P

LOCAL = 8
B = 128
SLOTS = 12
PAIRS = 36
RANKS = ("y", "x", "zl", "zh", "core")
RING = ("zl", "zh", "core")
PLANE = ("y", "x")


def pair_place(a, b):
    return a * (a + 1) // 2 + b


def is_odd():
    return lax.axis_index("core") == 1


def mark_kernel(count, ocol, basis, sent, sem):
    fetch = pltpu.make_async_copy(basis, sent.at[pl.ds(0, LOCAL * B), :], sem)
    fetch.start()
    first = lax.axis_index(RANKS) * LOCAL
    row = lax.broadcasted_iota(jnp.int32, (2 * LOCAL, B), 0)
    lane = lax.broadcasted_iota(jnp.int32, (2 * LOCAL, B), 1)
    marks = jnp.zeros((2 * LOCAL, B), jnp.float32)
    for r in range(LOCAL):
        mark = lane < 0
        for s in range(SLOTS):
            mark = jnp.logical_or(mark, lane == lax.rem(ocol[r, s] - first + 2 * LOCAL + count, count))
        marks = jnp.where(jnp.logical_and(mark, row == r), 1.0, marks)
    sent[LOCAL * B :, :] = marks.astype(jnp.bfloat16)
    fetch.wait()


def mark(count, ocol, basis):
    return pl.pallas_call(
        functools.partial(mark_kernel, count),
        out_shape=jax.ShapeDtypeStruct((LOCAL * B + 2 * LOCAL, B), jnp.bfloat16),
        in_specs=[pl.BlockSpec(memory_space=pltpu.SMEM), pl.BlockSpec(memory_space=pl.ANY)],
        out_specs=pl.BlockSpec(memory_space=pltpu.VMEM),
        scratch_shapes=[pltpu.SemaphoreType.DMA],
        compiler_params=pltpu.CompilerParams(vmem_limit_bytes=56 * 1024 * 1024),
        name="mark",
    )(ocol, basis)


def pack_kernel(count, tcol, tval_hbm, to_far, to_near, table, tval, sem):
    fetch = pltpu.make_async_copy(tval_hbm, tval, sem)
    fetch.start()
    odd = is_odd()
    first = lax.axis_index(RANKS) * LOCAL
    far_right = jnp.where(odd, 0, PAIRS)
    far_left = PAIRS - far_right
    for p in range(2 * PAIRS):
        table[p] = 0
    for r in range(LOCAL):
        for s in range(SLOTS):
            v = lax.rem(tcol[r, s] - first + LOCAL + count, count)
            place = jnp.where(
                v >= 2 * LOCAL,
                far_right + pair_place(r, 0) + v - 2 * LOCAL,
                jnp.where(v < LOCAL, far_left + pair_place(LOCAL - 1 - r, 0) + LOCAL - 1 - v, 2 * PAIRS),
            )
            table[place] = s
    fetch.wait()
    for a in range(LOCAL):
        far_row = jnp.where(odd, a, LOCAL - 1 - a)
        near_row = LOCAL - 1 - far_row
        for b in range(a + 1):
            p = pair_place(a, b)
            to_far[:, p * B : (p + 1) * B] = tval[far_row, table[p]]
            to_near[:, p * B : (p + 1) * B] = tval[near_row, table[PAIRS + p]]


def pack(count, tcol, tval):
    out = jax.ShapeDtypeStruct((B, PAIRS * B), jnp.bfloat16)
    vmem = pl.BlockSpec(memory_space=pltpu.VMEM)
    return pl.pallas_call(
        functools.partial(pack_kernel, count),
        out_shape=(out, out),
        in_specs=[pl.BlockSpec(memory_space=pltpu.SMEM), pl.BlockSpec(memory_space=pl.ANY)],
        out_specs=(vmem, vmem),
        scratch_shapes=[
            pltpu.SMEM((2 * PAIRS + 1,), jnp.int32),
            pltpu.VMEM((LOCAL, SLOTS, B, B), jnp.bfloat16),
            pltpu.SemaphoreType.DMA,
        ],
        compiler_params=pltpu.CompilerParams(vmem_limit_bytes=56 * 1024 * 1024),
        name="pack",
    )(tcol, tval)


def inner_kernel(tcol, wanted, held, tval, basis_far, basis, basis_near, y_out, p_out, level, basis_t, blocks, z, y_own, t_own, table):
    odd = is_odd()
    size = LOCAL * B
    far_at = jnp.where(odd, 2 * size, 0)
    blocks[pl.ds(pl.multiple_of(far_at, size), size), :] = basis_far[:size, :]
    blocks[size : 2 * size, :] = basis[...]
    blocks[pl.ds(pl.multiple_of(2 * size - far_at, size), size), :] = basis_near[:size, :]
    for p in range(LOCAL * LOCAL):
        table[p] = 0
    for r in range(LOCAL):
        for s in range(SLOTS):
            v = tcol[LOCAL + r, s] - LOCAL
            inside = jnp.logical_and(v >= 0, v < LOCAL)
            table[jnp.where(inside, r * LOCAL + v, LOCAL * LOCAL)] = s

    @pl.loop(0, LOCAL)
    def _(j):
        for s in range(SLOTS):
            c = tcol[LOCAL + j, s]
            z[s] = jnp.dot(
                tval[j, s],
                blocks[pl.ds(pl.multiple_of(c * B, B), B), :],
                preferred_element_type=jnp.float32,
            )

        @pl.loop(0, 2 * LOCAL + 1)
        def _(d):
            i = j + d
            r = i & (LOCAL - 1)
            part = i >> 3
            own = part == 1
            left = part == 0
            a = jnp.where(left, r, LOCAL - 1 - r)
            b = jnp.where(left, j, LOCAL - 1 - j)
            place = (a * (a + 1) >> 1) + b + jnp.where(left == odd, PAIRS, 0)
            place = jnp.where(own, r * LOCAL + j, place)
            rows = pl.ds(pl.multiple_of(place * B, B), B)
            on = held[i, j]

            def total():
                y = jnp.zeros((B, B), jnp.float32)
                for s in range(SLOTS):
                    y = y + wanted[i, tcol[LOCAL + j, s]] * z[s]
                return y.astype(jnp.bfloat16)

            @pl.when(jnp.logical_and(own, on == 1))
            def _():
                y_own[rows, :] = total()

            @pl.when(jnp.logical_and(jnp.logical_not(own), on == 1))
            def _():
                y_out[rows, :] = total()

            @pl.when(jnp.logical_and(own, on == 0))
            def _():
                y_own[rows, :] = jnp.zeros((B, B), jnp.bfloat16)

            @pl.when(jnp.logical_and(jnp.logical_not(own), on == 0))
            def _():
                y_out[rows, :] = jnp.zeros((B, B), jnp.bfloat16)

    level[...] = jnp.zeros((B, B), jnp.float32)

    for r in range(LOCAL):
        for j in range(LOCAL):
            t_own[r % 2, :, j * B : (j + 1) * B] = tval[r, table[r * LOCAL + j]]
        size = LOCAL * B
        p = jnp.dot(
            t_own[r % 2], y_own[r * size : (r + 1) * size, :], preferred_element_type=jnp.float32
        )
        rows = slice(r * B, (r + 1) * B)
        p_out[rows, :] = p
        level[...] += lax.dot_general(
            basis[rows, :], p.astype(jnp.bfloat16), (((0,), (0,)), ((), ())), preferred_element_type=jnp.float32
        )

    for part, ref in enumerate((basis_far, basis_near)):
        for r in range(LOCAL):
            place = (part * LOCAL + r) * B
            basis_t[:, place : place + B] = ref[r * B : (r + 1) * B, :].T


def inner(tcol, wanted, held, tval, basis_far, basis, basis_near):
    vmem = pl.BlockSpec(memory_space=pltpu.VMEM)
    smem = pl.BlockSpec(memory_space=pltpu.SMEM)
    return pl.pallas_call(
        inner_kernel,
        out_shape=(
            jax.ShapeDtypeStruct((2 * PAIRS * B, B), jnp.bfloat16),
            jax.ShapeDtypeStruct((LOCAL * B, B), jnp.float32),
            jax.ShapeDtypeStruct((B, B), jnp.float32),
            jax.ShapeDtypeStruct((B, 2 * LOCAL * B), jnp.bfloat16),
        ),
        in_specs=[smem, smem, smem, vmem, vmem, vmem, vmem],
        out_specs=(vmem, vmem, vmem, vmem),
        scratch_shapes=[
            pltpu.VMEM((3 * LOCAL * B, B), jnp.bfloat16),
            pltpu.VMEM((SLOTS, B, B), jnp.float32),
            pltpu.VMEM((LOCAL * LOCAL * B, B), jnp.bfloat16),
            pltpu.VMEM((2, B, LOCAL * B), jnp.bfloat16),
            pltpu.SMEM((LOCAL * LOCAL + 1,), jnp.int32),
        ],
        compiler_params=pltpu.CompilerParams(vmem_limit_bytes=28 * 1024 * 1024),
        cost_estimate=pl.CostEstimate(flops=12_000_000_000, bytes_accessed=8_000_000, transcendentals=0),
        name="inner",
    )(tcol, wanted, held, tval, basis_far, basis, basis_near)


def outer_kernel(side, received, y, basis_t, level_in, p_out, level):
    odd = is_odd()
    for a in range(LOCAL):
        at = pair_place(a, 0) * B
        span = (a + 1) * B
        row = jnp.where(odd == (side == 0), LOCAL - 1 - a, a)
        p = jnp.dot(received[:, at : at + span], y[at : at + span, :], preferred_element_type=jnp.float32)
        p_out[pl.ds(pl.multiple_of(row * B, B), B), :] = p.astype(jnp.bfloat16)
    level[...] = level_in[...] + jnp.dot(basis_t[...], p_out[...], preferred_element_type=jnp.float32)


def outer(side, received, y, basis_t, level, name):
    vmem = pl.BlockSpec(memory_space=pltpu.VMEM)
    rows = LOCAL * B
    return pl.pallas_call(
        functools.partial(outer_kernel, side),
        grid=(1,),
        out_shape=(jax.ShapeDtypeStruct((rows, B), jnp.bfloat16), jax.ShapeDtypeStruct((B, B), jnp.float32)),
        in_specs=[
            vmem,
            pl.BlockSpec((PAIRS * B, B), lambda i: (side, 0)),
            pl.BlockSpec((B, rows), lambda i: (0, side)),
            vmem,
        ],
        out_specs=(vmem, vmem),
        compiler_params=pltpu.CompilerParams(vmem_limit_bytes=20 * 1024 * 1024),
        cost_estimate=pl.CostEstimate(flops=400_000_000, bytes_accessed=3_000_000, transcendentals=0),
        name=name,
    )(received, y, basis_t, level)


def copies(part, count):
    return jnp.broadcast_to(part[None], (count,) + part.shape)


def per_device(tval, tcol, ocol, basis):
    devices = lax.axis_size(RANKS)
    count = LOCAL * devices
    me = lax.axis_index(RANKS)
    first = me * LOCAL
    near = [(i, i ^ 1) for i in range(devices)]
    far = [(i, (i + 1) % devices if i % 2 else (i - 1) % devices) for i in range(devices)]
    ring = lax.axis_size(RING)
    plane = lax.axis_size(PLANE)

    cols = jnp.concatenate(
        [lax.dynamic_slice_in_dim(tcol, ((me + k) % devices) * LOCAL, LOCAL, 0) for k in (devices - 1, 0, 1)]
    )
    cols = (cols - first + LOCAL + count) % count
    sent = mark(count, ocol, basis)
    basis_far = lax.ppermute(sent, RANKS, far)
    basis_near = lax.ppermute(sent, RANKS, near)
    to_far, to_near = pack(count, lax.dynamic_slice_in_dim(tcol, first, LOCAL, 0), tval)
    from_far = lax.ppermute(to_far, RANKS, far)
    from_near = lax.ppermute(to_near, RANKS, near)

    held = jnp.any(cols[:, :, None] == LOCAL + jnp.arange(LOCAL, dtype=jnp.int32), axis=1).astype(jnp.int32)
    rows = LOCAL * B
    odd = is_odd()
    far_marks, near_marks = (part[rows : rows + LOCAL] for part in (basis_far, basis_near))
    wanted = jnp.concatenate(
        [
            jnp.where(odd, near_marks, far_marks)[:, 2 * LOCAL : 5 * LOCAL],
            sent[rows : rows + LOCAL, LOCAL : 4 * LOCAL],
            jnp.where(odd, far_marks, near_marks)[:, : 3 * LOCAL],
        ]
    ).astype(jnp.float32)
    y, p_own, level, basis_t = inner(cols, wanted, held, tval, basis_far, basis, basis_near)
    p_near, level = outer(1, from_near, y, basis_t, level, "outer_near")
    p_far, level = outer(0, from_far, y, basis_t, level, "outer_far")

    theirs_far = lax.ppermute(p_far, RANKS, far)
    theirs_near = lax.ppermute(p_near, RANKS, near)

    level = lax.all_to_all(level.reshape(ring, B // ring, B), RING, 0, 0).sum(0)
    level = lax.all_to_all(copies(level, plane), PLANE, 0, 0).sum(0)
    level = level / jnp.sqrt(jnp.float32(count * B))
    level = lax.all_to_all(copies(level, ring), RING, 0, 0).reshape(B, B)

    projected = p_own + theirs_far.astype(jnp.float32) + theirs_near.astype(jnp.float32)
    return (projected.astype(jnp.bfloat16), level)


def solution(mesh):
    mesh = Mesh(mesh.devices.reshape(8, 4, 2, 4, 2), RANKS)
    return jax.shard_map(
        per_device,
        mesh=mesh,
        in_specs=(P(RANKS, None, None, None), P(), P(RANKS, None), P(RANKS, None)),
        out_specs=(P(RANKS, None), P()),
        check_vma=False,
    )
```

time: 179 us -> 106 us (0.59)
  Pallas kernels: 96 us -> 30 us
  blocking collectives: 17.7 us -> 10.2 us
  starting transfers between devices: 41.3 us -> 48.2 us
  waiting for transfers between devices: 12.9 us -> 9.91 us
  other arithmetic: 4.24 us -> 1.65 us
    pallas_call x2 -> x4, Pallas kernels: 77 us -> 11.2 us  [the longest x1 4.73 us: pack(): pl.pallas_call(functools.partial(pack_kernel, count), out_shape=(out, out...]
    all_to_all x1, blocking collectives: 17.7 us -> 10.2 us  [per_device(): level = lax.all_to_all(level.reshape(ring, B // ring, B), RING, 0, 0).sum(0)]
    ppermute x6, starting transfers between devices: 27.3 us -> 32.1 us  [the longest x1 11.7 us: per_device(): basis_near = lax.ppermute(sent, RANKS, near)]
    all_to_all x1, waiting for transfers between devices: 4.81 us -> 0.68 us  [per_device(): level = lax.all_to_all(copies(level, plane), PLANE, 0, 0).sum(0)]
    all_to_all x1, starting transfers between devices: 8.54 us -> 10.8 us  [per_device(): level = lax.all_to_all(copies(level, plane), PLANE, 0, 0).sum(0)]
    concatenate x1 -> x0, other arithmetic: 1.88 us -> none  [per_device(): sent = jnp.concatenate([basis, mine, jnp.zeros_like(mine)], axis=0)]
  transfers between devices with their start and end apart: 8 -> 8, of which waited for: 3 -> 3; matrix products, arithmetic and copies ran while one was open for 3% -> 5% of each run, Pallas kernels for 52% -> 24%
where the time goes in v2:
time: 106 us
  starting transfers between devices  48.2 us (45%)
  Pallas kernels  30 us (28%)
  blocking collectives  10.2 us (10%)
  waiting for transfers between devices  9.91 us (9%)
  local copies, waits for them, and re-layouts  4.77 us (4%)
  other arithmetic  1.65 us (2%)
    pallas_call x1, Pallas kernels, inner(): pl.pallas_call(inner_kernel, out_shape=(jax.ShapeDtypeStruct((2 * PAIRS *...  18.8 us
    ppermute x1, starting transfers between devices, per_device(): basis_near = lax.ppermute(sent, RANKS, near)  11.7 us
    all_to_all x1, starting transfers between devices, per_device(): level = lax.all_to_all(copies(level, plane), PLANE, 0, 0).sum(0)  10.8 us
    all_to_all x1, blocking collectives, per_device(): level = lax.all_to_all(level.reshape(ring, B // ring, B), RING, 0, 0).sum(0)  10.2 us
    ppermute x1, starting transfers between devices, per_device(): basis_far = lax.ppermute(sent, RANKS, far)  7.2 us
    all_to_all x1, waiting for transfers between devices, per_device(): level = lax.all_to_all(copies(level, ring), RING, 0, 0).reshape(B, B)  7 us
    ppermute x1, starting transfers between devices, per_device(): theirs_near = lax.ppermute(p_near, RANKS, near)  6.05 us
    all_to_all x1, starting transfers between devices, per_device(): level = lax.all_to_all(copies(level, ring), RING, 0, 0).reshape(B, B)  5.24 us
  transfers between devices with their start and end apart: 8, of which 3 were waited for; matrix products, arithmetic and copies ran while one was open for 5% of the time, Pallas kernels for 24%

profile of v2, /device:TPU:1, one launch (start us, length us, event | category | flops | bytes accessed | tf_op | source)
XLA Modules:
  0.0 105.6 jit_solution(11037426921500647890)
XLA Ops:
  0.6 2.4 %mark.1 = bf16[1040,128]{1,0:T(8,128)(2,1)} custom-call(s32[8,12]{1,0:T(8,128)} %ocol.1, bf16[1024,128]{1,0:T(8,128)(2,1)} %basis.3), custom_call_target="tpu_custom_call" | custom-call | tf_op jit(solution)/shard_map/mark/pallas_call | solution.py:45
  3.0 7.2 %collective-permute-start.1 = (bf16[1040,128]{1,0:T(8,128)(2,1)}, bf16[1040,128]{1,0:T(8,128)(2,1)}, u32[]{:S(2)}, u32[]{:S(2)}) collective-permute-start(bf16[1040,128]{1,0:T(8,128)(2,1)} %mark.1), channel_id=1, source_target_pairs={{0,511},{1,2},{2,1},{3,4},{4,3},{5,6},{6,5},{7,8},{8,7},{9,10},{10... | collective-permute-start | bytes 798728 | tf_op jit(solution)/shard_map/ppermute | solution.py:260
  10.2 11.7 %collective-permute-start = (bf16[1040,128]{1,0:T(8,128)(2,1)}, bf16[1040,128]{1,0:T(8,128)(2,1)}, u32[]{:S(2)}, u32[]{:S(2)}) collective-permute-start(bf16[1040,128]{1,0:T(8,128)(2,1)} %mark.1), channel_id=1, source_target_pairs={{0,1},{1,0},{2,3},{3,2},{4,5},{5,4},{6,7},{7,6},{8,9},{9,8},{10,11... | collective-permute-start | bytes 798728 | tf_op jit(solution)/shard_map/ppermute | solution.py:261
  22.0 0.0 copy-start.3
  22.0 0.9 constant_dynamic-slice_fusion.3
  22.9 0.7 copy.25.tcol
  23.6 0.0 copy-start
  23.6 4.7 %pack.1 = (bf16[128,4608]{1,0:T(8,128)(2,1)}, bf16[128,4608]{1,0:T(8,128)(2,1)}) custom-call(s32[8,12]{1,0:T(8,128)} %copy.25.tcol, bf16[8,12,128,128]{3,2,1,0:T(8,128)(2,1)} %tval_hbm.1), custom_call_target="tpu_custom_call" | custom-call | tf_op jit(solution)/shard_map/pack/pallas_call | solution.py:87
  28.4 1.9 %collective-permute-start.2 = (bf16[128,4608]{1,0:T(8,128)(2,1)}, bf16[128,4608]{1,0:T(8,128)(2,1)}, u32[]{:S(2)}, u32[]{:S(2)}) collective-permute-start(bf16[128,4608]{1,0:T(8,128)(2,1)} %get-tuple-element.13), channel_id=1, source_target_pairs={{0,511},{1,2},{2,1},{3,4},{4,3},{5,6},{6,5},{7,8},{8,7},{9,10},{10... | collective-permute-start | bytes 3538952 | tf_op jit(solution)/shard_map/ppermute | solution.py:263
  30.3 2.6 %collective-permute-start.3 = (bf16[128,4608]{1,0:T(8,128)(2,1)}, bf16[128,4608]{1,0:T(8,128)(2,1)}, u32[]{:S(2)}, u32[]{:S(2)}) collective-permute-start(bf16[128,4608]{1,0:T(8,128)(2,1)} %get-tuple-element.16), channel_id=1, source_target_pairs={{0,1},{1,0},{2,3},{3,2},{4,5},{5,4},{6,7},{7,6},{8,9},{9,8},{10,11... | collective-permute-start | bytes 3538952 | tf_op jit(solution)/shard_map/ppermute | solution.py:264
  32.8 0.1 copy.22
  32.9 0.1 copy.24
  33.0 0.1 copy.23
  33.1 0.7 slice.22
  33.8 0.1 copy.19
  33.9 0.1 compare_reduce_fusion
  34.0 0.1 copy.20.held
  34.1 0.0 collective-permute-done.1.basis_far
  34.1 0.0 collective-permute-done.basis_near
  34.1 0.7 broadcast_select_fusion.1
  34.8 0.1 slice.17
  34.9 0.0 copy-done.3
  34.9 0.0 copy-done
  34.9 18.8 %inner.1 = (bf16[9216,128]{1,0:T(8,128)(2,1)S(1)}, f32[1024,128]{1,0:T(8,128)S(1)}, f32[128,128]{1,0:T(8,128)S(1)}, bf16[128,2048]{1,0:T(8,128)(2,1)S(1)}) custom-call(s32[24,12]{1,0:T(8,128)S(1)} %add_select_fusion.tcol, f32[24,24]{1,0:T(8,128)S(1)} %maximum_convert_fusion.wanted, s32[24,8]{1,0:T(8,128)S(1)} %copy.20.held, ...), custom_call_target="tpu_custom_call" | custom-call | flops 12000000000 | bytes 8000000 | tf_op jit(solution)/shard_map/inner/pallas_call | solution.py:187
  53.7 0.0 copy-start.1
  53.7 0.0 collective-permute-done.3.received
  53.7 2.1 %outer_near.1 = (bf16[1024,128]{1,0:T(8,128)(2,1)S(1)}, f32[128,128]{1,0:T(8,128)S(1)}) custom-call(bf16[128,4608]{1,0:T(8,128)(2,1)} %collective-permute-done.3.received, bf16[9216,128]{1,0:T(8,128)(2,1)S(1)} %get-tuple-element.14.y, bf16[128,2048]{1,0:T(8,128)(2,1)S(1)} %get-tuple-element.15.basis_t, f32[128,128]{1,0:T(8,128)S(1)} %get-tuple-element.17.level_in), custom_call_target="tpu_custom_call" | custom-call | flops 400000000 | bytes 3000000 | tf_op jit(solution)/shard_map/outer_near/pallas_call | solution.py:224
  55.8 0.0 copy-done.1
  55.8 2.2 %collective-permute-done.2.received = bf16[128,4608]{1,0:T(8,128)(2,1)} collective-permute-done((bf16[128,4608]{1,0:T(8,128)(2,1)}, bf16[128,4608]{1,0:T(8,128)(2,1)}, u32[]{:S(2)}, u32[]{:S(2)}) %collective-permute-start.2) | collective-permute-done | bytes 1179680 | tf_op jit(solution)/shard_map/ppermute | solution.py:263
  58.1 2.0 %outer_far.1 = (bf16[1024,128]{1,0:T(8,128)(2,1)S(1)}, f32[128,128]{1,0:T(8,128)S(1)}) custom-call(bf16[128,4608]{1,0:T(8,128)(2,1)} %collective-permute-done.2.received, bf16[9216,128]{1,0:T(8,128)(2,1)S(1)} %get-tuple-element.14.y, bf16[128,2048]{1,0:T(8,128)(2,1)S(1)} %get-tuple-element.15.basis_t, f32[128,128]{1,0:T(8,128)S(1)} %get-tuple-element.18.level_in), custom_call_target="tpu_custom_call" | custom-call | flops 400000000 | bytes 3000000 | tf_op jit(solution)/shard_map/outer_far/pallas_call | solution.py:224
  60.0 0.0 copy-start.2
  60.0 10.2 %all_to_all.15 = f32[16,8,128]{2,1,0:T(8,128)S(1)} all-to-all(f32[16,8,128]{2,1,0:T(8,128)S(1)} %bitcast.3), channel_id=1, replica_groups=mesh['y'=8,'x'=4,'zl'=2,'zh'=4,'core'=2] {'zl','zh','core'}, dimensions={0} | all-to-all | bytes 131072 | tf_op jit(solution)/shard_map/all_to_all | solution.py:284
  70.3 0.7 broadcast_in_dim.4
  70.9 10.8 %all-to-all-start.1 = ((f32[32,8,128]{2,1,0:T(8,128)}), f32[32,8,128]{2,1,0:T(8,128)S(1)}, u32[]{:S(2)}, u32[]{:S(2)}) async-start(f32[32,8,128]{2,1,0:T(8,128)} %broadcast_in_dim.4), calls=%async_computation.1 | async-start | bytes 262144 | tf_op jit(solution)/shard_map/all_to_all | solution.py:285
  81.8 2.7 %collective-permute-start.4 = (bf16[1024,128]{1,0:T(8,128)(2,1)S(1)}, bf16[1024,128]{1,0:T(8,128)(2,1)S(1)}, u32[]{:S(2)}, u32[]{:S(2)}) collective-permute-start(bf16[1024,128]{1,0:T(8,128)(2,1)S(1)} %get-tuple-element.19), channel_id=1, source_target_pairs={{0,511},{1,2},{2,1},{3,4},{4,3},{5,6},{6,5},{7,8},{8,7},{9,10},{10... | collective-permute-start | bytes 786440 | tf_op jit(solution)/shard_map/ppermute | solution.py:281
  84.5 6.0 %collective-permute-start.5 = (bf16[1024,128]{1,0:T(8,128)(2,1)S(1)}, bf16[1024,128]{1,0:T(8,128)(2,1)S(1)}, u32[]{:S(2)}, u32[]{:S(2)}) collective-permute-start(bf16[1024,128]{1,0:T(8,128)(2,1)S(1)} %get-tuple-element.20), channel_id=1, source_target_pairs={{0,1},{1,0},{2,3},{3,2},{4,5},{5,4},{6,7},{7,6},{8,9},{9,8},{10,11... | collective-permute-start | bytes 786440 | tf_op jit(solution)/shard_map/ppermute | solution.py:282
  90.5 0.7 all-to-all-done.1
  91.3 0.6 broadcast_in_dim.5
  91.9 5.2 %all-to-all-start.2 = ((f32[16,8,128]{2,1,0:T(8,128)}), f32[16,8,128]{2,1,0:T(8,128)S(1)}, u32[]{:S(2)}, u32[]{:S(2)}) async-start(f32[16,8,128]{2,1,0:T(8,128)} %broadcast_in_dim.5), calls=%async_computation.2 | async-start | bytes 131072 | tf_op jit(solution)/shard_map/all_to_all | solution.py:287
  97.1 0.0 collective-permute-done.4
  97.2 0.0 collective-permute-done.5
  97.2 0.0 copy-done.2
  97.2 0.8 add_convert_fusion
  98.0 7.0 %all-to-all-done.2 = f32[16,8,128]{2,1,0:T(8,128)S(1)} async-done(((f32[16,8,128]{2,1,0:T(8,128)}), f32[16,8,128]{2,1,0:T(8,128)S(1)}, u32[]{:S(2)}, u32[]{:S(2)}) %all-to-all-start.2) | async-done | bytes 65568 | tf_op jit(solution)/shard_map/all_to_all | solution.py:287
  105.0 0.6 copy.27
  (7 shorter events, 0.1 us)
Async XLA Ops:
  3.0 31.1 %collective-permute-start.1 = (bf16[1040,128]{1,0:T(8,128)(2,1)}, bf16[1040,128]{1,0:T(8,128)(2,1)}, u32[]{:S(2)}, u32[]{:S(2)}) collective-permute-start(bf16[1040,128]{1,0:T(8,128)(2,1)} %mark.1), channel_id=1, source_target_pairs={{0,511},{1,2},{2,1},{3,4},{4,3},{5,6},{6,5},{7,8},{8,7},{9,10},{10... | collective-permute-start | bytes 798728 | tf_op jit(solution)/shard_map/ppermute | solution.py:260
  10.2 23.9 %collective-permute-start = (bf16[1040,128]{1,0:T(8,128)(2,1)}, bf16[1040,128]{1,0:T(8,128)(2,1)}, u32[]{:S(2)}, u32[]{:S(2)}) collective-permute-start(bf16[1040,128]{1,0:T(8,128)(2,1)} %mark.1), channel_id=1, source_target_pairs={{0,1},{1,0},{2,3},{3,2},{4,5},{5,4},{6,7},{7,6},{8,9},{9,8},{10,11... | collective-permute-start | bytes 798728 | tf_op jit(solution)/shard_map/ppermute | solution.py:261
  22.0 12.9 %copy-start.3 = (bf16[1024,128]{1,0:T(8,128)(2,1)S(1)}, bf16[1024,128]{1,0:T(8,128)(2,1)}, u32[]{:S(2)}) copy-start(bf16[1024,128]{1,0:T(8,128)(2,1)} %basis.3) | copy-start | bytes 786436
  23.6 11.3 %copy-start = (bf16[8,12,128,128]{3,2,1,0:T(8,128)(2,1)S(1)}, bf16[8,12,128,128]{3,2,1,0:T(8,128)(2,1)}, u32[]{:S(2)}) copy-start(bf16[8,12,128,128]{3,2,1,0:T(8,128)(2,1)} %tval_hbm.1) | copy-start | bytes 9437188
  28.4 29.7 %collective-permute-start.2 = (bf16[128,4608]{1,0:T(8,128)(2,1)}, bf16[128,4608]{1,0:T(8,128)(2,1)}, u32[]{:S(2)}, u32[]{:S(2)}) collective-permute-start(bf16[128,4608]{1,0:T(8,128)(2,1)} %get-tuple-element.13), channel_id=1, source_target_pairs={{0,511},{1,2},{2,1},{3,4},{4,3},{5,6},{6,5},{7,8},{8,7},{9,10},{10... | collective-permute-start | bytes 3538952 | tf_op jit(solution)/shard_map/ppermute | solution.py:263
  30.3 23.4 %collective-permute-start.3 = (bf16[128,4608]{1,0:T(8,128)(2,1)}, bf16[128,4608]{1,0:T(8,128)(2,1)}, u32[]{:S(2)}, u32[]{:S(2)}) collective-permute-start(bf16[128,4608]{1,0:T(8,128)(2,1)} %get-tuple-element.16), channel_id=1, source_target_pairs={{0,1},{1,0},{2,3},{3,2},{4,5},{5,4},{6,7},{7,6},{8,9},{9,8},{10,11... | collective-permute-start | bytes 3538952 | tf_op jit(solution)/shard_map/ppermute | solution.py:264
  53.7 2.2 %copy-start.1 = (f32[1024,128]{1,0:T(8,128)}, f32[1024,128]{1,0:T(8,128)S(1)}, u32[]{:S(2)}) copy-start(f32[1024,128]{1,0:T(8,128)S(1)} %get-tuple-element.12) | copy-start | bytes 1572868
  60.0 37.1 %copy-start.2 = (f32[1024,128]{1,0:T(8,128)S(1)}, f32[1024,128]{1,0:T(8,128)}, u32[]{:S(2)}) copy-start(f32[1024,128]{1,0:T(8,128)} %copy-done.1) | copy-start | bytes 1572868
  70.9 20.3 %all-to-all-start.1 = ((f32[32,8,128]{2,1,0:T(8,128)}), f32[32,8,128]{2,1,0:T(8,128)S(1)}, u32[]{:S(2)}, u32[]{:S(2)}) async-start(f32[32,8,128]{2,1,0:T(8,128)} %broadcast_in_dim.4), calls=%async_computation.1 | async-start | bytes 262144 | tf_op jit(solution)/shard_map/all_to_all | solution.py:285
  81.8 15.4 %collective-permute-start.4 = (bf16[1024,128]{1,0:T(8,128)(2,1)S(1)}, bf16[1024,128]{1,0:T(8,128)(2,1)S(1)}, u32[]{:S(2)}, u32[]{:S(2)}) collective-permute-start(bf16[1024,128]{1,0:T(8,128)(2,1)S(1)} %get-tuple-element.19), channel_id=1, source_target_pairs={{0,511},{1,2},{2,1},{3,4},{4,3},{5,6},{6,5},{7,8},{8,7},{9,10},{10... | collective-permute-start | bytes 786440 | tf_op jit(solution)/shard_map/ppermute | solution.py:281
  84.5 12.7 %collective-permute-start.5 = (bf16[1024,128]{1,0:T(8,128)(2,1)S(1)}, bf16[1024,128]{1,0:T(8,128)(2,1)S(1)}, u32[]{:S(2)}, u32[]{:S(2)}) collective-permute-start(bf16[1024,128]{1,0:T(8,128)(2,1)S(1)} %get-tuple-element.20), channel_id=1, source_target_pairs={{0,1},{1,0},{2,3},{3,2},{4,5},{5,4},{6,7},{7,6},{8,9},{9,8},{10,11... | collective-permute-start | bytes 786440 | tf_op jit(solution)/shard_map/ppermute | solution.py:282
  91.9 13.1 %all-to-all-start.2 = ((f32[16,8,128]{2,1,0:T(8,128)}), f32[16,8,128]{2,1,0:T(8,128)S(1)}, u32[]{:S(2)}, u32[]{:S(2)}) async-start(f32[16,8,128]{2,1,0:T(8,128)} %broadcast_in_dim.5), calls=%async_computation.2 | async-start | bytes 131072 | tf_op jit(solution)/shard_map/all_to_all | solution.py:287

commit v3 on v2

--- a/solution.py
+++ b/solution.py
@@ -282,7 +282,7 @@
     theirs_near = lax.ppermute(p_near, RANKS, near)
 
     level = lax.all_to_all(level.reshape(ring, B // ring, B), RING, 0, 0).sum(0)
-    level = lax.all_to_all(copies(level, plane), PLANE, 0, 0).sum(0)
+    level = lax.all_to_all(copies(level.astype(jnp.bfloat16), plane), PLANE, 0, 0).astype(jnp.float32).sum(0)
     level = level / jnp.sqrt(jnp.float32(count * B))
     level = lax.all_to_all(copies(level, ring), RING, 0, 0).reshape(B, B)
 

time: 106 us -> 105 us (level)
  transfers between devices with their start and end apart: 8 -> 8, of which waited for: 3 -> 2; matrix products, arithmetic and copies ran while one was open for 5% -> 5% of each run, Pallas kernels for 24% -> 24%
where the time goes in v3:
time: 105 us
  starting transfers between devices  47.9 us (46%)
  Pallas kernels  29.9 us (28%)
  blocking collectives  10.1 us (10%)
  waiting for transfers between devices  9.41 us (9%)
  local copies, waits for them, and re-layouts  4.74 us (5%)
  other arithmetic  1.65 us (2%)
    pallas_call x1, Pallas kernels, inner(): pl.pallas_call(inner_kernel, out_shape=(jax.ShapeDtypeStruct((2 * PAIRS *...  18.7 us
    ppermute x1, starting transfers between devices, per_device(): basis_near = lax.ppermute(sent, RANKS, near)  11.7 us
    all_to_all x1, starting transfers between devices, per_device(): lax.all_to_all(copies(level.astype(jnp.bfloat16), plane), PLANE, 0, 0)  10.8 us
    all_to_all x1, blocking collectives, per_device(): level = lax.all_to_all(level.reshape(ring, B // ring, B), RING, 0, 0).sum(0)  10.1 us
    ppermute x1, starting transfers between devices, per_device(): basis_far = lax.ppermute(sent, RANKS, far)  7.2 us
    all_to_all x1, waiting for transfers between devices, per_device(): level = lax.all_to_all(copies(level, ring), RING, 0, 0).reshape(B, B)  7 us
    ppermute x1, starting transfers between devices, per_device(): theirs_near = lax.ppermute(p_near, RANKS, near)  6.05 us
    all_to_all x1, starting transfers between devices, per_device(): level = lax.all_to_all(copies(level, ring), RING, 0, 0).reshape(B, B)  4.99 us
  transfers between devices with their start and end apart: 8, of which 2 were waited for; matrix products, arithmetic and copies ran while one was open for 5% of the time, Pallas kernels for 24%

profile of v3, /device:TPU:1, one launch (start us, length us, event | category | flops | bytes accessed | tf_op | source)
XLA Modules:
  0.0 104.6 jit_solution(17061866688150477192)
XLA Ops:
  0.6 2.4 %mark.1 = bf16[1040,128]{1,0:T(8,128)(2,1)} custom-call(s32[8,12]{1,0:T(8,128)} %ocol.1, bf16[1024,128]{1,0:T(8,128)(2,1)} %basis.3), custom_call_target="tpu_custom_call" | custom-call | tf_op jit(solution)/shard_map/mark/pallas_call | solution.py:45
  3.0 7.2 %collective-permute-start.1 = (bf16[1040,128]{1,0:T(8,128)(2,1)}, bf16[1040,128]{1,0:T(8,128)(2,1)}, u32[]{:S(2)}, u32[]{:S(2)}) collective-permute-start(bf16[1040,128]{1,0:T(8,128)(2,1)} %mark.1), channel_id=1, source_target_pairs={{0,511},{1,2},{2,1},{3,4},{4,3},{5,6},{6,5},{7,8},{8,7},{9,10},{10... | collective-permute-start | bytes 798728 | tf_op jit(solution)/shard_map/ppermute | solution.py:260
  10.2 11.7 %collective-permute-start = (bf16[1040,128]{1,0:T(8,128)(2,1)}, bf16[1040,128]{1,0:T(8,128)(2,1)}, u32[]{:S(2)}, u32[]{:S(2)}) collective-permute-start(bf16[1040,128]{1,0:T(8,128)(2,1)} %mark.1), channel_id=1, source_target_pairs={{0,1},{1,0},{2,3},{3,2},{4,5},{5,4},{6,7},{7,6},{8,9},{9,8},{10,11... | collective-permute-start | bytes 798728 | tf_op jit(solution)/shard_map/ppermute | solution.py:261
  22.0 0.0 copy-start.3
  22.0 0.9 constant_dynamic-slice_fusion.3
  22.9 0.7 copy.25.tcol
  23.6 0.0 copy-start
  23.6 4.7 %pack.1 = (bf16[128,4608]{1,0:T(8,128)(2,1)}, bf16[128,4608]{1,0:T(8,128)(2,1)}) custom-call(s32[8,12]{1,0:T(8,128)} %copy.25.tcol, bf16[8,12,128,128]{3,2,1,0:T(8,128)(2,1)} %tval_hbm.1), custom_call_target="tpu_custom_call" | custom-call | tf_op jit(solution)/shard_map/pack/pallas_call | solution.py:87
  28.4 1.9 %collective-permute-start.2 = (bf16[128,4608]{1,0:T(8,128)(2,1)}, bf16[128,4608]{1,0:T(8,128)(2,1)}, u32[]{:S(2)}, u32[]{:S(2)}) collective-permute-start(bf16[128,4608]{1,0:T(8,128)(2,1)} %get-tuple-element.13), channel_id=1, source_target_pairs={{0,511},{1,2},{2,1},{3,4},{4,3},{5,6},{6,5},{7,8},{8,7},{9,10},{10... | collective-permute-start | bytes 3538952 | tf_op jit(solution)/shard_map/ppermute | solution.py:263
  30.3 2.6 %collective-permute-start.3 = (bf16[128,4608]{1,0:T(8,128)(2,1)}, bf16[128,4608]{1,0:T(8,128)(2,1)}, u32[]{:S(2)}, u32[]{:S(2)}) collective-permute-start(bf16[128,4608]{1,0:T(8,128)(2,1)} %get-tuple-element.16), channel_id=1, source_target_pairs={{0,1},{1,0},{2,3},{3,2},{4,5},{5,4},{6,7},{7,6},{8,9},{9,8},{10,11... | collective-permute-start | bytes 3538952 | tf_op jit(solution)/shard_map/ppermute | solution.py:264
  32.8 0.1 copy.22
  32.9 0.1 copy.24
  33.0 0.1 copy.23
  33.1 0.7 slice.22
  33.8 0.1 copy.19
  33.9 0.1 compare_reduce_fusion
  34.0 0.1 copy.20.held
  34.1 0.0 collective-permute-done.1.basis_far
  34.1 0.0 collective-permute-done.basis_near
  34.1 0.7 broadcast_select_fusion.1
  34.8 0.1 slice.17
  34.9 0.0 copy-done.3
  34.9 0.0 copy-done
  34.9 18.7 %inner.1 = (bf16[9216,128]{1,0:T(8,128)(2,1)S(1)}, f32[1024,128]{1,0:T(8,128)S(1)}, f32[128,128]{1,0:T(8,128)S(1)}, bf16[128,2048]{1,0:T(8,128)(2,1)S(1)}) custom-call(s32[24,12]{1,0:T(8,128)S(1)} %add_select_fusion.tcol, f32[24,24]{1,0:T(8,128)S(1)} %maximum_convert_fusion.wanted, s32[24,8]{1,0:T(8,128)S(1)} %copy.20.held, ...), custom_call_target="tpu_custom_call" | custom-call | flops 12000000000 | bytes 8000000 | tf_op jit(solution)/shard_map/inner/pallas_call | solution.py:187
  53.5 0.0 copy-start.1
  53.5 0.0 collective-permute-done.3.received
  53.6 2.1 %outer_near.1 = (bf16[1024,128]{1,0:T(8,128)(2,1)S(1)}, f32[128,128]{1,0:T(8,128)S(1)}) custom-call(bf16[128,4608]{1,0:T(8,128)(2,1)} %collective-permute-done.3.received, bf16[9216,128]{1,0:T(8,128)(2,1)S(1)} %get-tuple-element.14.y, bf16[128,2048]{1,0:T(8,128)(2,1)S(1)} %get-tuple-element.15.basis_t, f32[128,128]{1,0:T(8,128)S(1)} %get-tuple-element.17.level_in), custom_call_target="tpu_custom_call" | custom-call | flops 400000000 | bytes 3000000 | tf_op jit(solution)/shard_map/outer_near/pallas_call | solution.py:224
  55.7 0.0 copy-done.1
  55.7 2.4 %collective-permute-done.2.received = bf16[128,4608]{1,0:T(8,128)(2,1)} collective-permute-done((bf16[128,4608]{1,0:T(8,128)(2,1)}, bf16[128,4608]{1,0:T(8,128)(2,1)}, u32[]{:S(2)}, u32[]{:S(2)}) %collective-permute-start.2) | collective-permute-done | bytes 1179680 | tf_op jit(solution)/shard_map/ppermute | solution.py:263
  58.1 0.0 copy-start.2
  58.1 2.0 %outer_far.1 = (bf16[1024,128]{1,0:T(8,128)(2,1)S(1)}, f32[128,128]{1,0:T(8,128)S(1)}) custom-call(bf16[128,4608]{1,0:T(8,128)(2,1)} %collective-permute-done.2.received, bf16[9216,128]{1,0:T(8,128)(2,1)S(1)} %get-tuple-element.14.y, bf16[128,2048]{1,0:T(8,128)(2,1)S(1)} %get-tuple-element.15.basis_t, f32[128,128]{1,0:T(8,128)S(1)} %get-tuple-element.18.level_in), custom_call_target="tpu_custom_call" | custom-call | flops 400000000 | bytes 3000000 | tf_op jit(solution)/shard_map/outer_far/pallas_call | solution.py:224
  60.1 10.1 %all_to_all.15 = f32[16,8,128]{2,1,0:T(8,128)S(1)} all-to-all(f32[16,8,128]{2,1,0:T(8,128)S(1)} %bitcast.3), channel_id=1, replica_groups=mesh['y'=8,'x'=4,'zl'=2,'zh'=4,'core'=2] {'zl','zh','core'}, dimensions={0} | all-to-all | bytes 131072 | tf_op jit(solution)/shard_map/all_to_all | solution.py:284
  70.2 0.6 broadcast_in_dim.4
  70.9 10.8 %all-to-all-start.1 = ((bf16[32,8,128]{2,1,0:T(8,128)(2,1)}), bf16[32,8,128]{2,1,0:T(8,128)(2,1)S(1)}, u32[]{:S(2)}, u32[]{:S(2)}) async-start(bf16[32,8,128]{2,1,0:T(8,128)(2,1)} %broadcast_in_dim.4), calls=%async_computation.1 | async-start | bytes 131072 | tf_op jit(solution)/shard_map/all_to_all | solution.py:285
  81.7 2.7 %collective-permute-start.4 = (bf16[1024,128]{1,0:T(8,128)(2,1)S(1)}, bf16[1024,128]{1,0:T(8,128)(2,1)S(1)}, u32[]{:S(2)}, u32[]{:S(2)}) collective-permute-start(bf16[1024,128]{1,0:T(8,128)(2,1)S(1)} %get-tuple-element.19), channel_id=1, source_target_pairs={{0,511},{1,2},{2,1},{3,4},{4,3},{5,6},{6,5},{7,8},{8,7},{9,10},{10... | collective-permute-start | bytes 786440 | tf_op jit(solution)/shard_map/ppermute | solution.py:281
  84.4 6.0 %collective-permute-start.5 = (bf16[1024,128]{1,0:T(8,128)(2,1)S(1)}, bf16[1024,128]{1,0:T(8,128)(2,1)S(1)}, u32[]{:S(2)}, u32[]{:S(2)}) collective-permute-start(bf16[1024,128]{1,0:T(8,128)(2,1)S(1)} %get-tuple-element.20), channel_id=1, source_target_pairs={{0,1},{1,0},{2,3},{3,2},{4,5},{5,4},{6,7},{7,6},{8,9},{9,8},{10,11... | collective-permute-start | bytes 786440 | tf_op jit(solution)/shard_map/ppermute | solution.py:282
  90.5 0.0 all-to-all-done.1
  90.5 0.6 broadcast_in_dim.5
  91.2 5.0 %all-to-all-start.2 = ((f32[16,8,128]{2,1,0:T(8,128)}), f32[16,8,128]{2,1,0:T(8,128)S(1)}, u32[]{:S(2)}, u32[]{:S(2)}) async-start(f32[16,8,128]{2,1,0:T(8,128)} %broadcast_in_dim.5), calls=%async_computation.2 | async-start | bytes 131072 | tf_op jit(solution)/shard_map/all_to_all | solution.py:287
  96.2 0.0 collective-permute-done.4
  96.2 0.0 collective-permute-done.5
  96.2 0.0 copy-done.2
  96.2 0.8 add_convert_fusion
  97.0 7.0 %all-to-all-done.2 = f32[16,8,128]{2,1,0:T(8,128)S(1)} async-done(((f32[16,8,128]{2,1,0:T(8,128)}), f32[16,8,128]{2,1,0:T(8,128)S(1)}, u32[]{:S(2)}, u32[]{:S(2)}) %all-to-all-start.2) | async-done | bytes 65568 | tf_op jit(solution)/shard_map/all_to_all | solution.py:287
  104.0 0.6 copy.27
  (7 shorter events, 0.1 us)
Async XLA Ops:
  3.0 31.1 %collective-permute-start.1 = (bf16[1040,128]{1,0:T(8,128)(2,1)}, bf16[1040,128]{1,0:T(8,128)(2,1)}, u32[]{:S(2)}, u32[]{:S(2)}) collective-permute-start(bf16[1040,128]{1,0:T(8,128)(2,1)} %mark.1), channel_id=1, source_target_pairs={{0,511},{1,2},{2,1},{3,4},{4,3},{5,6},{6,5},{7,8},{8,7},{9,10},{10... | collective-permute-start | bytes 798728 | tf_op jit(solution)/shard_map/ppermute | solution.py:260
  10.2 23.9 %collective-permute-start = (bf16[1040,128]{1,0:T(8,128)(2,1)}, bf16[1040,128]{1,0:T(8,128)(2,1)}, u32[]{:S(2)}, u32[]{:S(2)}) collective-permute-start(bf16[1040,128]{1,0:T(8,128)(2,1)} %mark.1), channel_id=1, source_target_pairs={{0,1},{1,0},{2,3},{3,2},{4,5},{5,4},{6,7},{7,6},{8,9},{9,8},{10,11... | collective-permute-start | bytes 798728 | tf_op jit(solution)/shard_map/ppermute | solution.py:261
  22.0 12.9 %copy-start.3 = (bf16[1024,128]{1,0:T(8,128)(2,1)S(1)}, bf16[1024,128]{1,0:T(8,128)(2,1)}, u32[]{:S(2)}) copy-start(bf16[1024,128]{1,0:T(8,128)(2,1)} %basis.3) | copy-start | bytes 786436
  23.6 11.3 %copy-start = (bf16[8,12,128,128]{3,2,1,0:T(8,128)(2,1)S(1)}, bf16[8,12,128,128]{3,2,1,0:T(8,128)(2,1)}, u32[]{:S(2)}) copy-start(bf16[8,12,128,128]{3,2,1,0:T(8,128)(2,1)} %tval_hbm.1) | copy-start | bytes 9437188
  28.4 29.7 %collective-permute-start.2 = (bf16[128,4608]{1,0:T(8,128)(2,1)}, bf16[128,4608]{1,0:T(8,128)(2,1)}, u32[]{:S(2)}, u32[]{:S(2)}) collective-permute-start(bf16[128,4608]{1,0:T(8,128)(2,1)} %get-tuple-element.13), channel_id=1, source_target_pairs={{0,511},{1,2},{2,1},{3,4},{4,3},{5,6},{6,5},{7,8},{8,7},{9,10},{10... | collective-permute-start | bytes 3538952 | tf_op jit(solution)/shard_map/ppermute | solution.py:263
  30.3 23.3 %collective-permute-start.3 = (bf16[128,4608]{1,0:T(8,128)(2,1)}, bf16[128,4608]{1,0:T(8,128)(2,1)}, u32[]{:S(2)}, u32[]{:S(2)}) collective-permute-start(bf16[128,4608]{1,0:T(8,128)(2,1)} %get-tuple-element.16), channel_id=1, source_target_pairs={{0,1},{1,0},{2,3},{3,2},{4,5},{5,4},{6,7},{7,6},{8,9},{9,8},{10,11... | collective-permute-start | bytes 3538952 | tf_op jit(solution)/shard_map/ppermute | solution.py:264
  53.5 2.2 %copy-start.1 = (f32[1024,128]{1,0:T(8,128)}, f32[1024,128]{1,0:T(8,128)S(1)}, u32[]{:S(2)}) copy-start(f32[1024,128]{1,0:T(8,128)S(1)} %get-tuple-element.12) | copy-start | bytes 1572868
  58.1 38.1 %copy-start.2 = (f32[1024,128]{1,0:T(8,128)S(1)}, f32[1024,128]{1,0:T(8,128)}, u32[]{:S(2)}) copy-start(f32[1024,128]{1,0:T(8,128)} %copy-done.1) | copy-start | bytes 1572868
  70.9 19.6 %all-to-all-start.1 = ((bf16[32,8,128]{2,1,0:T(8,128)(2,1)}), bf16[32,8,128]{2,1,0:T(8,128)(2,1)S(1)}, u32[]{:S(2)}, u32[]{:S(2)}) async-start(bf16[32,8,128]{2,1,0:T(8,128)(2,1)} %broadcast_in_dim.4), calls=%async_computation.1 | async-start | bytes 131072 | tf_op jit(solution)/shard_map/all_to_all | solution.py:285
  81.7 14.5 %collective-permute-start.4 = (bf16[1024,128]{1,0:T(8,128)(2,1)S(1)}, bf16[1024,128]{1,0:T(8,128)(2,1)S(1)}, u32[]{:S(2)}, u32[]{:S(2)}) collective-permute-start(bf16[1024,128]{1,0:T(8,128)(2,1)S(1)} %get-tuple-element.19), channel_id=1, source_target_pairs={{0,511},{1,2},{2,1},{3,4},{4,3},{5,6},{6,5},{7,8},{8,7},{9,10},{10... | collective-permute-start | bytes 786440 | tf_op jit(solution)/shard_map/ppermute | solution.py:281
  84.4 11.8 %collective-permute-start.5 = (bf16[1024,128]{1,0:T(8,128)(2,1)S(1)}, bf16[1024,128]{1,0:T(8,128)(2,1)S(1)}, u32[]{:S(2)}, u32[]{:S(2)}) collective-permute-start(bf16[1024,128]{1,0:T(8,128)(2,1)S(1)} %get-tuple-element.20), channel_id=1, source_target_pairs={{0,1},{1,0},{2,3},{3,2},{4,5},{5,4},{6,7},{7,6},{8,9},{9,8},{10,11... | collective-permute-start | bytes 786440 | tf_op jit(solution)/shard_map/ppermute | solution.py:282
  91.2 12.8 %all-to-all-start.2 = ((f32[16,8,128]{2,1,0:T(8,128)}), f32[16,8,128]{2,1,0:T(8,128)S(1)}, u32[]{:S(2)}, u32[]{:S(2)}) async-start(f32[16,8,128]{2,1,0:T(8,128)} %broadcast_in_dim.5), calls=%async_computation.2 | async-start | bytes 131072 | tf_op jit(solution)/shard_map/all_to_all | solution.py:287

commit v4 on v3

--- a/solution.py
+++ b/solution.py
@@ -207,7 +207,8 @@
     )(tcol, wanted, held, tval, basis_far, basis, basis_near)
 
 
-def outer_kernel(side, received, y, basis_t, level_in, p_out, level):
+def outer_kernel(side, received, y, basis_t, level_in, earlier, p_out, level):
+    del earlier
     odd = is_odd()
     for a in range(LOCAL):
         at = pair_place(a, 0) * B
@@ -218,7 +219,7 @@
     level[...] = level_in[...] + jnp.dot(basis_t[...], p_out[...], preferred_element_type=jnp.float32)
 
 
-def outer(side, received, y, basis_t, level, name):
+def outer(side, received, y, basis_t, level, earlier, name):
     vmem = pl.BlockSpec(memory_space=pltpu.VMEM)
     rows = LOCAL * B
     return pl.pallas_call(
@@ -230,12 +231,13 @@
             pl.BlockSpec((PAIRS * B, B), lambda i: (side, 0)),
             pl.BlockSpec((B, rows), lambda i: (0, side)),
             vmem,
+            pl.BlockSpec(memory_space=pl.ANY),
         ],
         out_specs=(vmem, vmem),
         compiler_params=pltpu.CompilerParams(vmem_limit_bytes=20 * 1024 * 1024),
         cost_estimate=pl.CostEstimate(flops=400_000_000, bytes_accessed=3_000_000, transcendentals=0),
         name=name,
-    )(received, y, basis_t, level)
+    )(received, y, basis_t, level, earlier)
 
 
 def copies(part, count):
@@ -275,11 +277,11 @@
         ]
     ).astype(jnp.float32)
     y, p_own, level, basis_t = inner(cols, wanted, held, tval, basis_far, basis, basis_near)
-    p_near, level = outer(1, from_near, y, basis_t, level, "outer_near")
-    p_far, level = outer(0, from_far, y, basis_t, level, "outer_far")
+    p_near, level = outer(1, from_near, y, basis_t, level, level, "outer_near")
+    theirs_near = lax.ppermute(p_near, RANKS, near)
+    p_far, level = outer(0, from_far, y, basis_t, level, theirs_near, "outer_far")
 
     theirs_far = lax.ppermute(p_far, RANKS, far)
-    theirs_near = lax.ppermute(p_near, RANKS, near)
 
     level = lax.all_to_all(level.reshape(ring, B // ring, B), RING, 0, 0).sum(0)
     level = lax.all_to_all(copies(level.astype(jnp.bfloat16), plane), PLANE, 0, 0).astype(jnp.float32).sum(0)

time: 105 us -> 105 us (level)
  starting transfers between devices: 47.9 us -> 41.5 us
  waiting for transfers between devices: 9.41 us -> 14.6 us
  blocking collectives: 10.1 us -> 11.4 us
    all_to_all x1, waiting for transfers between devices: 0.04 us -> 6.1 us  [per_device(): lax.all_to_all(copies(level.astype(jnp.bfloat16), plane), PLANE, 0, 0)]
    ppermute x1, starting transfers between devices: 6.05 us -> 1.92 us  [per_device(): theirs_near = lax.ppermute(p_near, RANKS, near)]
    all_to_all x1, starting transfers between devices: 10.8 us -> 8.5 us  [per_device(): lax.all_to_all(copies(level.astype(jnp.bfloat16), plane), PLANE, 0, 0)]
    ppermute x1, waiting for transfers between devices: 2.36 us -> 0.48 us  [per_device(): from_far = lax.ppermute(to_far, RANKS, far)]
    all_to_all x1, blocking collectives: 10.1 us -> 11.4 us  [per_device(): level = lax.all_to_all(level.reshape(ring, B // ring, B), RING, 0, 0).sum(0)]
  transfers between devices with their start and end apart: 8 -> 8, of which waited for: 2 -> 4; matrix products, arithmetic and copies ran while one was open for 5% -> 5% of each run, Pallas kernels for 24% -> 24%
where the time goes in v4:
time: 105 us
  starting transfers between devices  41.5 us (40%)
  Pallas kernels  29.9 us (28%)
  waiting for transfers between devices  14.6 us (14%)
  blocking collectives  11.4 us (11%)
  local copies, waits for them, and re-layouts  4.74 us (5%)
  other arithmetic  1.65 us (2%)
    pallas_call x1, Pallas kernels, inner(): pl.pallas_call(inner_kernel, out_shape=(jax.ShapeDtypeStruct((2 * PAIRS *...  18.6 us
    ppermute x1, starting transfers between devices, per_device(): basis_near = lax.ppermute(sent, RANKS, near)  11.7 us
    all_to_all x1, blocking collectives, per_device(): level = lax.all_to_all(level.reshape(ring, B // ring, B), RING, 0, 0).sum(0)  11.4 us
    all_to_all x1, starting transfers between devices, per_device(): lax.all_to_all(copies(level.astype(jnp.bfloat16), plane), PLANE, 0, 0)  8.5 us
    ppermute x1, starting transfers between devices, per_device(): basis_far = lax.ppermute(sent, RANKS, far)  7.2 us
    all_to_all x1, waiting for transfers between devices, per_device(): level = lax.all_to_all(copies(level, ring), RING, 0, 0).reshape(B, B)  7.01 us
    all_to_all x1, waiting for transfers between devices, per_device(): lax.all_to_all(copies(level.astype(jnp.bfloat16), plane), PLANE, 0, 0)  6.1 us
    all_to_all x1, starting transfers between devices, per_device(): level = lax.all_to_all(copies(level, ring), RING, 0, 0).reshape(B, B)  4.99 us
  transfers between devices with their start and end apart: 8, of which 4 were waited for; matrix products, arithmetic and copies ran while one was open for 5% of the time, Pallas kernels for 24%

profile of v4, /device:TPU:1, one launch (start us, length us, event | category | flops | bytes accessed | tf_op | source)
XLA Modules:
  0.0 104.6 jit_solution(5435699583010728173)
XLA Ops:
  0.6 2.4 %mark.1 = bf16[1040,128]{1,0:T(8,128)(2,1)} custom-call(s32[8,12]{1,0:T(8,128)} %ocol.1, bf16[1024,128]{1,0:T(8,128)(2,1)} %basis.3), custom_call_target="tpu_custom_call" | custom-call | tf_op jit(solution)/shard_map/mark/pallas_call | solution.py:45
  3.0 7.2 %collective-permute-start.1 = (bf16[1040,128]{1,0:T(8,128)(2,1)}, bf16[1040,128]{1,0:T(8,128)(2,1)}, u32[]{:S(2)}, u32[]{:S(2)}) collective-permute-start(bf16[1040,128]{1,0:T(8,128)(2,1)} %mark.1), channel_id=1, source_target_pairs={{0,511},{1,2},{2,1},{3,4},{4,3},{5,6},{6,5},{7,8},{8,7},{9,10},{10... | collective-permute-start | bytes 798728 | tf_op jit(solution)/shard_map/ppermute | solution.py:262
  10.2 11.7 %collective-permute-start = (bf16[1040,128]{1,0:T(8,128)(2,1)}, bf16[1040,128]{1,0:T(8,128)(2,1)}, u32[]{:S(2)}, u32[]{:S(2)}) collective-permute-start(bf16[1040,128]{1,0:T(8,128)(2,1)} %mark.1), channel_id=1, source_target_pairs={{0,1},{1,0},{2,3},{3,2},{4,5},{5,4},{6,7},{7,6},{8,9},{9,8},{10,11... | collective-permute-start | bytes 798728 | tf_op jit(solution)/shard_map/ppermute | solution.py:263
  22.0 0.0 copy-start.3
  22.0 0.9 constant_dynamic-slice_fusion.3
  22.9 0.7 copy.25.tcol
  23.6 0.0 copy-start
  23.6 4.7 %pack.1 = (bf16[128,4608]{1,0:T(8,128)(2,1)}, bf16[128,4608]{1,0:T(8,128)(2,1)}) custom-call(s32[8,12]{1,0:T(8,128)} %copy.25.tcol, bf16[8,12,128,128]{3,2,1,0:T(8,128)(2,1)} %tval_hbm.1), custom_call_target="tpu_custom_call" | custom-call | tf_op jit(solution)/shard_map/pack/pallas_call | solution.py:87
  28.4 1.9 %collective-permute-start.2 = (bf16[128,4608]{1,0:T(8,128)(2,1)}, bf16[128,4608]{1,0:T(8,128)(2,1)}, u32[]{:S(2)}, u32[]{:S(2)}) collective-permute-start(bf16[128,4608]{1,0:T(8,128)(2,1)} %get-tuple-element.13), channel_id=1, source_target_pairs={{0,511},{1,2},{2,1},{3,4},{4,3},{5,6},{6,5},{7,8},{8,7},{9,10},{10... | collective-permute-start | bytes 3538952 | tf_op jit(solution)/shard_map/ppermute | solution.py:265
  30.3 2.6 %collective-permute-start.3 = (bf16[128,4608]{1,0:T(8,128)(2,1)}, bf16[128,4608]{1,0:T(8,128)(2,1)}, u32[]{:S(2)}, u32[]{:S(2)}) collective-permute-start(bf16[128,4608]{1,0:T(8,128)(2,1)} %get-tuple-element.16), channel_id=1, source_target_pairs={{0,1},{1,0},{2,3},{3,2},{4,5},{5,4},{6,7},{7,6},{8,9},{9,8},{10,11... | collective-permute-start | bytes 3538952 | tf_op jit(solution)/shard_map/ppermute | solution.py:266
  32.8 0.1 copy.22
  32.9 0.1 copy.24
  33.0 0.1 copy.23
  33.1 0.7 slice.22
  33.8 0.1 copy.19
  33.9 0.1 compare_reduce_fusion
  34.0 0.1 copy.20.held
  34.1 0.0 collective-permute-done.1.basis_far
  34.1 0.0 collective-permute-done.basis_near
  34.1 0.7 broadcast_select_fusion.1
  34.8 0.1 slice.17
  34.9 0.0 copy-done.3
  34.9 0.0 copy-done
  34.9 18.6 %inner.1 = (bf16[9216,128]{1,0:T(8,128)(2,1)S(1)}, f32[1024,128]{1,0:T(8,128)S(1)}, f32[128,128]{1,0:T(8,128)S(1)}, bf16[128,2048]{1,0:T(8,128)(2,1)S(1)}) custom-call(s32[24,12]{1,0:T(8,128)S(1)} %add_select_fusion.tcol, f32[24,24]{1,0:T(8,128)S(1)} %maximum_convert_fusion.wanted, s32[24,8]{1,0:T(8,128)S(1)} %copy.20.held, ...), custom_call_target="tpu_custom_call" | custom-call | flops 12000000000 | bytes 8000000 | tf_op jit(solution)/shard_map/inner/pallas_call | solution.py:187
  53.5 0.0 copy-start.1
  53.5 0.0 collective-permute-done.3.received
  53.5 2.1 %outer_near.1 = (bf16[1024,128]{1,0:T(8,128)(2,1)S(1)}, f32[128,128]{1,0:T(8,128)S(1)}) custom-call(bf16[128,4608]{1,0:T(8,128)(2,1)} %collective-permute-done.3.received, bf16[9216,128]{1,0:T(8,128)(2,1)S(1)} %get-tuple-element.14.y, bf16[128,2048]{1,0:T(8,128)(2,1)S(1)} %get-tuple-element.15.basis_t, f32[128,128]{1,0:T(8,128)S(1)} %get-tuple-element.17.level_in.earlier, ...), custom_call_target="tpu_custom_call" | custom-call | flops 400000000 | bytes 3000000 | tf_op jit(solution)/shard_map/outer_near/pallas_call | solution.py:225
  55.6 0.0 copy-done.1
  55.6 1.9 %collective-permute-start.4 = (bf16[1024,128]{1,0:T(8,128)(2,1)S(1)}, bf16[1024,128]{1,0:T(8,128)(2,1)S(1)}, u32[]{:S(2)}, u32[]{:S(2)}) collective-permute-start(bf16[1024,128]{1,0:T(8,128)(2,1)S(1)} %get-tuple-element.19), channel_id=1, source_target_pairs={{0,1},{1,0},{2,3},{3,2},{4,5},{5,4},{6,7},{7,6},{8,9},{9,8},{10,11... | collective-permute-start | bytes 786440 | tf_op jit(solution)/shard_map/ppermute | solution.py:281
  57.6 0.5 collective-permute-done.2.received
  58.1 1.0 collective-permute-done.4.earlier
  59.1 0.0 copy-start.2
  59.1 2.0 %outer_far.1 = (bf16[1024,128]{1,0:T(8,128)(2,1)S(1)}, f32[128,128]{1,0:T(8,128)S(1)}) custom-call(bf16[128,4608]{1,0:T(8,128)(2,1)} %collective-permute-done.2.received, bf16[9216,128]{1,0:T(8,128)(2,1)S(1)} %get-tuple-element.14.y, bf16[128,2048]{1,0:T(8,128)(2,1)S(1)} %get-tuple-element.15.basis_t, f32[128,128]{1,0:T(8,128)S(1)} %get-tuple-element.18.level_in, ...), custom_call_target="tpu_custom_call" | custom-call | flops 400000000 | bytes 3000000 | tf_op jit(solution)/shard_map/outer_far/pallas_call | solution.py:225
  61.1 11.4 %all_to_all.15 = f32[16,8,128]{2,1,0:T(8,128)S(1)} all-to-all(f32[16,8,128]{2,1,0:T(8,128)S(1)} %bitcast.3), channel_id=1, replica_groups=mesh['y'=8,'x'=4,'zl'=2,'zh'=4,'core'=2] {'zl','zh','core'}, dimensions={0} | all-to-all | bytes 131072 | tf_op jit(solution)/shard_map/all_to_all | solution.py:286
  72.5 0.6 broadcast_in_dim.4
  73.2 8.5 %all-to-all-start.1 = ((bf16[32,8,128]{2,1,0:T(8,128)(2,1)}), bf16[32,8,128]{2,1,0:T(8,128)(2,1)S(1)}, u32[]{:S(2)}, u32[]{:S(2)}) async-start(bf16[32,8,128]{2,1,0:T(8,128)(2,1)} %broadcast_in_dim.4), calls=%async_computation.1 | async-start | bytes 131072 | tf_op jit(solution)/shard_map/all_to_all | solution.py:287
  81.7 2.7 %collective-permute-start.5 = (bf16[1024,128]{1,0:T(8,128)(2,1)S(1)}, bf16[1024,128]{1,0:T(8,128)(2,1)S(1)}, u32[]{:S(2)}, u32[]{:S(2)}) collective-permute-start(bf16[1024,128]{1,0:T(8,128)(2,1)S(1)} %get-tuple-element.20), channel_id=1, source_target_pairs={{0,511},{1,2},{2,1},{3,4},{4,3},{5,6},{6,5},{7,8},{8,7},{9,10},{10... | collective-permute-start | bytes 786440 | tf_op jit(solution)/shard_map/ppermute | solution.py:284
  84.4 6.1 %all-to-all-done.1 = bf16[32,8,128]{2,1,0:T(8,128)(2,1)S(1)} async-done(((bf16[32,8,128]{2,1,0:T(8,128)(2,1)}), bf16[32,8,128]{2,1,0:T(8,128)(2,1)S(1)}, u32[]{:S(2)}, u32[]{:S(2)}) %all-to-all-start.1) | async-done | bytes 65568 | tf_op jit(solution)/shard_map/all_to_all | solution.py:287
  90.5 0.6 broadcast_in_dim.5
  91.2 5.0 %all-to-all-start.2 = ((f32[16,8,128]{2,1,0:T(8,128)}), f32[16,8,128]{2,1,0:T(8,128)S(1)}, u32[]{:S(2)}, u32[]{:S(2)}) async-start(f32[16,8,128]{2,1,0:T(8,128)} %broadcast_in_dim.5), calls=%async_computation.2 | async-start | bytes 131072 | tf_op jit(solution)/shard_map/all_to_all | solution.py:289
  96.2 0.0 collective-permute-done.5
  96.2 0.0 copy-done.2
  96.2 0.8 add_convert_fusion
  97.0 7.0 %all-to-all-done.2 = f32[16,8,128]{2,1,0:T(8,128)S(1)} async-done(((f32[16,8,128]{2,1,0:T(8,128)}), f32[16,8,128]{2,1,0:T(8,128)S(1)}, u32[]{:S(2)}, u32[]{:S(2)}) %all-to-all-start.2) | async-done | bytes 65568 | tf_op jit(solution)/shard_map/all_to_all | solution.py:289
  104.0 0.6 copy.27
  (7 shorter events, 0.1 us)
Async XLA Ops:
  3.0 31.1 %collective-permute-start.1 = (bf16[1040,128]{1,0:T(8,128)(2,1)}, bf16[1040,128]{1,0:T(8,128)(2,1)}, u32[]{:S(2)}, u32[]{:S(2)}) collective-permute-start(bf16[1040,128]{1,0:T(8,128)(2,1)} %mark.1), channel_id=1, source_target_pairs={{0,511},{1,2},{2,1},{3,4},{4,3},{5,6},{6,5},{7,8},{8,7},{9,10},{10... | collective-permute-start | bytes 798728 | tf_op jit(solution)/shard_map/ppermute | solution.py:262
  10.2 23.9 %collective-permute-start = (bf16[1040,128]{1,0:T(8,128)(2,1)}, bf16[1040,128]{1,0:T(8,128)(2,1)}, u32[]{:S(2)}, u32[]{:S(2)}) collective-permute-start(bf16[1040,128]{1,0:T(8,128)(2,1)} %mark.1), channel_id=1, source_target_pairs={{0,1},{1,0},{2,3},{3,2},{4,5},{5,4},{6,7},{7,6},{8,9},{9,8},{10,11... | collective-permute-start | bytes 798728 | tf_op jit(solution)/shard_map/ppermute | solution.py:263
  22.0 12.9 %copy-start.3 = (bf16[1024,128]{1,0:T(8,128)(2,1)S(1)}, bf16[1024,128]{1,0:T(8,128)(2,1)}, u32[]{:S(2)}) copy-start(bf16[1024,128]{1,0:T(8,128)(2,1)} %basis.3) | copy-start | bytes 786436
  23.6 11.3 %copy-start = (bf16[8,12,128,128]{3,2,1,0:T(8,128)(2,1)S(1)}, bf16[8,12,128,128]{3,2,1,0:T(8,128)(2,1)}, u32[]{:S(2)}) copy-start(bf16[8,12,128,128]{3,2,1,0:T(8,128)(2,1)} %tval_hbm.1) | copy-start | bytes 9437188
  28.4 29.7 %collective-permute-start.2 = (bf16[128,4608]{1,0:T(8,128)(2,1)}, bf16[128,4608]{1,0:T(8,128)(2,1)}, u32[]{:S(2)}, u32[]{:S(2)}) collective-permute-start(bf16[128,4608]{1,0:T(8,128)(2,1)} %get-tuple-element.13), channel_id=1, source_target_pairs={{0,511},{1,2},{2,1},{3,4},{4,3},{5,6},{6,5},{7,8},{8,7},{9,10},{10... | collective-permute-start | bytes 3538952 | tf_op jit(solution)/shard_map/ppermute | solution.py:265
  30.3 23.2 %collective-permute-start.3 = (bf16[128,4608]{1,0:T(8,128)(2,1)}, bf16[128,4608]{1,0:T(8,128)(2,1)}, u32[]{:S(2)}, u32[]{:S(2)}) collective-permute-start(bf16[128,4608]{1,0:T(8,128)(2,1)} %get-tuple-element.16), channel_id=1, source_target_pairs={{0,1},{1,0},{2,3},{3,2},{4,5},{5,4},{6,7},{7,6},{8,9},{9,8},{10,11... | collective-permute-start | bytes 3538952 | tf_op jit(solution)/shard_map/ppermute | solution.py:266
  53.5 2.2 %copy-start.1 = (f32[1024,128]{1,0:T(8,128)}, f32[1024,128]{1,0:T(8,128)S(1)}, u32[]{:S(2)}) copy-start(f32[1024,128]{1,0:T(8,128)S(1)} %get-tuple-element.12) | copy-start | bytes 1572868
  55.6 3.4 %collective-permute-start.4 = (bf16[1024,128]{1,0:T(8,128)(2,1)S(1)}, bf16[1024,128]{1,0:T(8,128)(2,1)S(1)}, u32[]{:S(2)}, u32[]{:S(2)}) collective-permute-start(bf16[1024,128]{1,0:T(8,128)(2,1)S(1)} %get-tuple-element.19), channel_id=1, source_target_pairs={{0,1},{1,0},{2,3},{3,2},{4,5},{5,4},{6,7},{7,6},{8,9},{9,8},{10,11... | collective-permute-start | bytes 786440 | tf_op jit(solution)/shard_map/ppermute | solution.py:281
  59.1 37.1 %copy-start.2 = (f32[1024,128]{1,0:T(8,128)S(1)}, f32[1024,128]{1,0:T(8,128)}, u32[]{:S(2)}) copy-start(f32[1024,128]{1,0:T(8,128)} %copy-done.1) | copy-start | bytes 1572868
  73.2 17.3 %all-to-all-start.1 = ((bf16[32,8,128]{2,1,0:T(8,128)(2,1)}), bf16[32,8,128]{2,1,0:T(8,128)(2,1)S(1)}, u32[]{:S(2)}, u32[]{:S(2)}) async-start(bf16[32,8,128]{2,1,0:T(8,128)(2,1)} %broadcast_in_dim.4), calls=%async_computation.1 | async-start | bytes 131072 | tf_op jit(solution)/shard_map/all_to_all | solution.py:287
  81.7 14.5 %collective-permute-start.5 = (bf16[1024,128]{1,0:T(8,128)(2,1)S(1)}, bf16[1024,128]{1,0:T(8,128)(2,1)S(1)}, u32[]{:S(2)}, u32[]{:S(2)}) collective-permute-start(bf16[1024,128]{1,0:T(8,128)(2,1)S(1)} %get-tuple-element.20), channel_id=1, source_target_pairs={{0,511},{1,2},{2,1},{3,4},{4,3},{5,6},{6,5},{7,8},{8,7},{9,10},{10... | collective-permute-start | bytes 786440 | tf_op jit(solution)/shard_map/ppermute | solution.py:284
  91.2 12.8 %all-to-all-start.2 = ((f32[16,8,128]{2,1,0:T(8,128)}), f32[16,8,128]{2,1,0:T(8,128)S(1)}, u32[]{:S(2)}, u32[]{:S(2)}) async-start(f32[16,8,128]{2,1,0:T(8,128)} %broadcast_in_dim.5), calls=%async_computation.2 | async-start | bytes 131072 | tf_op jit(solution)/shard_map/all_to_all | solution.py:289
